TPU v7x, 512 devices: a whole 4x8x8 slice. The times are simulated.
512 devices in a mesh: tm: 4 (over z_lo, core), height: 16 (over x, z_hi), group: 8 (over y).
Axes of the slice: x: 4, y: 8, z: 8 (z_hi: 4, z_lo: 2; z = z_hi * 2 + z_lo), core: 2. Of those that a mesh axis runs over, the one named last changes fastest.
Arguments:
- queries: bfloat16 [8, 8, 32, 32, 1536], P('group', 'tm', 'height'), may hold values from -5 to 5
- keys: bfloat16 [8, 8, 32, 32, 1536], P('group', 'tm', 'height'), may hold values from -5 to 5
- values: bfloat16 [8, 8, 32, 32, 1536], P('group', 'tm', 'height'), may hold values from -6 to 6
- window: int32 [12, 3], replicated, may hold values from 0 to 2, as said below
- adapter_down_factor: bfloat16 [1536, 64], P('height'), may hold values from -0.15625 to 0.15625
- adapter_up_factor: bfloat16 [64, 3072], P(None, 'height'), may hold values from -0.75 to 0.75
- stream: bfloat16 [8, 8, 32, 32, 3072], P('group', 'tm', 'height'), may hold values from -6 to 6
- modulation: float32 [8, 3, 3072], P('group'), may hold values from -3 to 3
- closing_weight: bfloat16 [3072, 64], replicated, may hold values from -0.109375 to 0.109375
- closing_bias: float32 [64], replicated, may hold values from -3 to 3
- latent: float32 [8, 8, 32, 2048], P('group', 'tm', 'height'), may hold values from -6 to 6
- next_latent_sample: float32 [8, 8, 32, 2048], P('group', 'tm', 'height'), may hold values from -12.5 to 12.5
- sampling_log_probability: float32 [8], P('group'), may hold values from -5 to -2, as said below
- advantage: float32 [8], P('group'), may hold values from -2 to 2, as said below
Outputs:
- gradient_down_factor: float32 [1536, 64], P('height')
- gradient_up_factor: float32 [64, 3072], P(None, 'height')
Inputs may be any that keep to these rules, and one draw needn't show every extreme that they name: `window`: every head reaches at most 1 frame, 1 row and 2 tiles either way; in every draw some head reaches 1 frame, some head 1 row and some head 2 tiles. `sampling_log_probability`: each value lies in -2.9 to -2.0 or in -5.0 to -4.1. A rollout's advantage is positive, 0.5 to 2, where its sampling log-probability is -2.9 or more, and negative, -2 to -0.5, where it is -4.1 or less.
All inputs are finite; a program needn't handle non-finite values.
Results may differ from a plain program's by a relative error of at most 0.01.
Values may be sent and summed in bfloat16 or wider, within the bound.
A program may use at most 64 MiB of HBM per device.

v0:
```python
import math

import jax
import jax.numpy as jnp
from jax import lax
from jax.sharding import PartitionSpec as P

TILE_W = 8


SAMPLER_STEP = -0.5
CLIP_RANGE = 0.2
NORM_EPS = 1e-06
HALF_LOG_TAU = 0.5 * math.log(2.0 * math.pi)


def padded(cells, sides, width):
    for axis, dim in sides:
        count = lax.axis_size(axis)
        ends = count - 1
        head = lax.slice_in_dim(cells, 0, width, axis=dim)
        tail = lax.slice_in_dim(cells, cells.shape[dim] - width, cells.shape[dim], axis=dim)
        cells = jnp.concatenate(
            [
                lax.ppermute(tail, axis, [(i, (i + 1) % count) for i in range(ends)]),
                cells,
                lax.ppermute(head, axis, [((i + 1) % count, i) for i in range(ends)]),
            ],
            axis=dim,
        )
    return cells


def tile_mask(window, gap_frame, gap_row, gap_tile, inside):
    return (
        (gap_frame[None] <= window[:, 0][:, None, None])
        & (gap_row[None] <= window[:, 1][:, None, None])
        & (gap_tile[None] <= window[:, 2][:, None, None])
        & inside[None, None, :]
    )


def position_grid(first, second, third):
    frame_idx, row_idx, col_idx = jnp.meshgrid(
        jnp.arange(first, dtype=jnp.int32),
        jnp.arange(second, dtype=jnp.int32),
        jnp.arange(third, dtype=jnp.int32),
        indexing="ij",
    )
    return (frame_idx.ravel(), row_idx.ravel(), col_idx.ravel())


def attend(query_block, key_block, value_block, allowed):
    scale = query_block.shape[-1] ** (-0.5)
    scores = (
        jnp.einsum("qhd,khd->hqk", query_block, key_block, preferred_element_type=jnp.float32)
        * scale
    )
    scores = jnp.where(allowed, scores, -1e30)
    row_max = jnp.max(scores, axis=-1, keepdims=True)
    expo_terms = jnp.where(allowed, jnp.exp(scores - row_max), 0.0)
    row_sum = jnp.sum(expo_terms, axis=-1, keepdims=True)
    weights = (expo_terms / row_sum).astype(jnp.bfloat16)
    mixed = jnp.einsum("hqk,khd->qhd", weights, value_block, preferred_element_type=jnp.float32)
    return mixed.astype(jnp.bfloat16)


def head_forward_pass(
    attention_result,
    flowing_rows,
    modulation,
    adapter_down_factor,
    adapter_up_factor,
    closing_weight,
    closing_bias,
):
    lowrank_update = jnp.dot(
        attention_result, adapter_down_factor, preferred_element_type=jnp.float32
    ).astype(jnp.bfloat16)
    adapter_result = jnp.dot(lowrank_update, adapter_up_factor, preferred_element_type=jnp.float32)
    hidden = flowing_rows.astype(jnp.float32) + modulation[0] * adapter_result
    centre = jnp.mean(hidden, axis=-1, keepdims=True)
    spread = jnp.mean((hidden - centre) ** 2, axis=-1, keepdims=True)
    inverse_deviation = lax.rsqrt(spread + NORM_EPS)
    normalized_rows = (hidden - centre) * inverse_deviation
    normed = (normalized_rows * (1.0 + modulation[2]) + modulation[1]).astype(jnp.bfloat16)
    predicted_velocity = (
        jnp.dot(normed, closing_weight, preferred_element_type=jnp.float32) + closing_bias
    )
    return (lowrank_update, normalized_rows, inverse_deviation, predicted_velocity)


def split_parts(wide):
    upper = wide.astype(jnp.bfloat16)
    remain = wide - upper.astype(jnp.float32)
    middle = remain.astype(jnp.bfloat16)
    lowest = (remain - middle.astype(jnp.float32)).astype(jnp.bfloat16)
    return (upper, middle, lowest)


def precise_product(parts, narrow, contract_part, contract_narrow, parts_first):
    dims = (((contract_part,), (contract_narrow,)), ((), ()))
    flipped = (((contract_narrow,), (contract_part,)), ((), ()))

    def single(piece):
        if parts_first:
            return lax.dot_general(piece, narrow, dims, preferred_element_type=jnp.float32)
        return lax.dot_general(narrow, piece, flipped, preferred_element_type=jnp.float32)

    return single(parts[0]) + (single(parts[1]) + single(parts[2]))


def reverse_pass(
    residual_rows,
    lowrank_update,
    normalized_rows,
    inverse_deviation,
    attention_result,
    modulation,
    adapter_up_factor,
    closing_weight,
):
    g_velocity = SAMPLER_STEP * residual_rows
    g_normed = precise_product(split_parts(g_velocity), closing_weight, 1, 1, True)
    g_normal = g_normed * (1.0 + modulation[2])
    g_hidden = inverse_deviation * (
        g_normal
        - jnp.mean(g_normal, axis=-1, keepdims=True)
        - normalized_rows * jnp.mean(g_normal * normalized_rows, axis=-1, keepdims=True)
    )
    gradient_output = modulation[0] * g_hidden
    output_pieces = split_parts(gradient_output)
    gradient_up_factor = precise_product(output_pieces, lowrank_update, 0, 0, False)
    gradient_lowrank = precise_product(output_pieces, adapter_up_factor, 1, 1, True)
    gradient_down_factor = precise_product(
        split_parts(gradient_lowrank), attention_result, 0, 0, False
    )
    return (gradient_down_factor, gradient_up_factor)


def slopes(log_prob, sampling_log_probability, advantage, count):

    def surrogate(value):
        ratio = jnp.exp(value - sampling_log_probability)
        return jnp.maximum(
            -advantage * ratio, -advantage * jnp.clip(ratio, 1.0 - CLIP_RANGE, 1.0 + CLIP_RANGE)
        )

    _, pull = jax.vjp(surrogate, log_prob)
    return pull(jnp.ones_like(log_prob) / count)[0]


def coefficient(partial_value, count, sampling_log_probability, advantage):
    fit_total = lax.psum(partial_value, ("tm", "height"))
    log_prob = -fit_total / (2.0 * count) - HALF_LOG_TAU
    return slopes(log_prob, sampling_log_probability[0], advantage[0], lax.axis_size("group"))


def body(
    queries,
    keys,
    values,
    window,
    adapter_down_factor,
    adapter_up_factor,
    stream,
    modulation,
    closing_weight,
    closing_bias,
    latent,
    next_latent_sample,
    sampling_log_probability,
    advantage,
):
    _, frames, row_count, col_count, feature_width = queries.shape
    head_count = window.shape[0]
    head_size = feature_width // head_count
    lat_width = closing_weight.shape[1]
    stacked = jnp.stack([keys[0], values[0]])
    rimmed = padded(stacked, (("tm", 1), ("height", 2)), 1)
    key_total = (frames + 2) * (row_count + 2) * col_count
    key_frame, key_row, key_col = position_grid(frames + 2, row_count + 2, col_count)
    query_frame, query_row, query_col = position_grid(frames, row_count, col_count)
    frame_global = lax.axis_index("tm") * frames - 1 + key_frame
    row_global = lax.axis_index("height") * row_count - 1 + key_row
    inside = (
        (frame_global >= 0)
        & (frame_global < frames * lax.axis_size("tm"))
        & (row_global >= 0)
        & (row_global < row_count * lax.axis_size("height"))
    )
    gap_frame = jnp.abs(query_frame[:, None] + 1 - key_frame[None, :])
    gap_row = jnp.abs(query_row[:, None] + 1 - key_row[None, :])
    gap_tile = jnp.abs(query_col[:, None] // TILE_W - key_col[None, :] // TILE_W)
    allowed = tile_mask(window, gap_frame, gap_row, gap_tile, inside)
    attention_result = attend(
        queries.reshape(-1, head_count, head_size),
        rimmed[0].reshape(key_total, head_count, head_size),
        rimmed[1].reshape(key_total, head_count, head_size),
        allowed,
    ).reshape(-1, feature_width)
    gathered_a, gathered_b = (
        lax.all_gather(adapter_down_factor, "height", axis=0, tiled=True),
        lax.all_gather(adapter_up_factor, "height", axis=1, tiled=True),
    )
    lowrank_update, normalized_rows, inverse_deviation, predicted_velocity = head_forward_pass(
        attention_result,
        stream.reshape(-1, stream.shape[-1]),
        modulation[0],
        gathered_a,
        gathered_b,
        closing_weight,
        closing_bias,
    )
    residue = next_latent_sample[0] - (
        latent[0]
        + SAMPLER_STEP * predicted_velocity.reshape(frames, row_count, col_count * lat_width)
    )
    partial_value = jnp.sum(residue * residue)
    count = (
        frames * row_count * col_count * lat_width * lax.axis_size("tm") * lax.axis_size("height")
    )
    slope_now = coefficient(partial_value, count, sampling_log_probability, advantage)
    gradient_down_factor, gradient_up_factor = reverse_pass(
        (slope_now * residue).reshape(-1, lat_width),
        lowrank_update,
        normalized_rows,
        inverse_deviation,
        attention_result,
        modulation[0],
        gathered_b,
        closing_weight,
    )
    shares = (
        lax.psum_scatter(gradient_down_factor, "height", scatter_dimension=0, tiled=True),
        lax.psum_scatter(gradient_up_factor, "height", scatter_dimension=1, tiled=True),
    )
    share_a, share_b = lax.psum((shares[0], shares[1]), ("tm", "group"))
    return (share_a, share_b)


def solution(mesh):
    return jax.shard_map(
        body,
        mesh=mesh,
        in_specs=(
            P("group", "tm", "height", None, None),
            P("group", "tm", "height", None, None),
            P("group", "tm", "height", None, None),
            P(),
            P("height", None),
            P(None, "height"),
            P("group", "tm", "height", None, None),
            P("group", None, None),
            P(),
            P(),
            P("group", "tm", "height", None),
            P("group", "tm", "height", None),
            P("group"),
            P("group"),
        ),
        out_specs=(P("height", None), P(None, "height")),
        check_vma=False,
    )
```

profile of v0, /device:TPU:1, one launch (start us, length us, event | category | flops | bytes accessed | tf_op | source)
XLA Modules:
  0.0 741.6 jit_solution(1337867280918920341)
XLA Ops:
  7.2 1.1 constant_dynamic-update-slice_fusion.1
  8.3 1.0 constant_dynamic-update-slice_fusion
  9.4 1.0 fusion.47
  10.4 5.4 collective-permute-start
  15.8 4.7 collective-permute-start.1
  21.0 1.1 reshape.306
  22.1 39.8 %all-gather = bf16[16,96,64]{1,2,0:T(8,128)(2,1)S(1)} all-gather(bf16[1,96,64]{1,2,0:T(8,128)(2,1)S(1)} %bitcast.82), channel_id=1, replica_groups=mesh['tm'=4,'height'=16,'group'=8] {'height'}, dimensions={0}, use_global_device_ids=true | all-gather | bytes 208896 | tf_op jit(solution)/shard_map/all_gather | solution.py:203
  62.5 36.1 %all-gather.1 = bf16[16,192,64]{1,2,0:T(8,128)(2,1)S(1)} all-gather(bf16[1,192,64]{1,2,0:T(8,128)(2,1)S(1)} %bitcast.81), channel_id=1, replica_groups=mesh['tm'=4,'height'=16,'group'=8] {'height'}, dimensions={0}, use_global_device_ids=true | all-gather | bytes 417792 | tf_op jit(solution)/shard_map/all_gather | solution.py:204
  100.9 0.7 copy.35
  101.7 0.8 subtract_abs_fusion.2
  102.5 1.0 subtract_abs_fusion
  103.9 4.0 collective-permute-start.2
  107.9 1.3 collective-permute-start.3
  109.9 17.4 %collective-permute-done.2 = bf16[2,4,1,32,1536]{4,3,2,1,0:T(8,128)(2,1)S(1)} collective-permute-done((bf16[2,4,1,32,1536]{4,3,2,1,0:T(8,128)(2,1)S(1)}, bf16[2,4,1,32,1536]{4,3,2,1,0:T(8,128)(2,1)S(1)}, u32[]{:S(2)}, u32[]{:S(2)}) %collective-permute-start.2) | collective-permute-done | bytes 786464 | tf_op jit(solution)/shard_map/ppermute | solution.py:25
  127.3 5.4 collective-permute-done.3
  133.1 1.4 fusion.45
  134.5 3.9 reshape_squeeze.7
  138.5 2.1 reshape_squeeze.6
  140.6 6.4 fusion.48
  147.0 3.7 fusion.11
  153.2 153.0 %psum.21 = f32[]{:T(128)} all-reduce(f32[]{:T(128)} %fusion.30), channel_id=1, replica_groups=mesh['tm'=4,'height'=16,'group'=8] {'tm','height'}, use_global_device_ids=true, to_apply=%region_5.6 | all-reduce | flops 1 | bytes 8 | tf_op jit(solution)/shard_map/psum | solution.py:154
  307.8 0.8 fusion.44
  308.7 1.3 multiply_multiply_fusion
  312.2 1.2 copy.38
  314.3 1.6 copy.40
  316.0 99.7 %reduce-scatter.7.cloned.1.call-done = f32[96,64]{1,0:T(8,128)} async-done(((f32[1536,64]{1,0:T(8,128)}), f32[96,64]{1,0:T(8,128)}) %reduce-scatter.7.cloned.1.call-update) | async-done | bytes 24592
  415.7 1.5 copy.39
  417.2 93.8 %reduce-scatter.9.cloned.1.call-done = f32[192,64]{1,0:T(8,128)} async-done(((f32[3072,64]{1,0:T(8,128)}), f32[192,64]{1,0:T(8,128)}) %reduce-scatter.9.cloned.1.call-update) | async-done | bytes 49168
  511.0 1.6 copy.41
  512.6 219.7 %all-reduce.3.cloned.1.call-done = (f32[96,64]{0,1:T(8,128)}, f32[64,192]{1,0:T(8,128)}) async-done(((f32[96,64]{0,1:T(8,128)}, f32[64,192]{1,0:T(8,128)}), (f32[96,64]{0,1:T(8,128)}, f32[64,192]{1,0:T(8,128)})) %all-reduce.3.cloned.1.call-update) | async-done | bytes 73744 | tf_op jit(solution)/shard_map/psum | solution.py:238
  732.2 1.4 copy.63
  733.6 1.5 copy.64
  (106 shorter events, 9.8 us)
Async XLA Ops:
  7.2 144.7 %copy-start = (bf16[3072,64]{0,1:T(8,128)(2,1)S(1)}, bf16[3072,64]{0,1:T(8,128)(2,1)}, u32[]{:S(2)}) copy-start(bf16[3072,64]{0,1:T(8,128)(2,1)} %param.22) | copy-start | bytes 1179652
  7.2 13.9 %copy-start.7 = (bf16[1,2,2,32,1536]{4,3,2,1,0:T(8,128)(2,1)S(1)}, bf16[1,2,2,32,1536]{4,3,2,1,0:T(8,128)(2,1)}, u32[]{:S(2)}) copy-start(bf16[1,2,2,32,1536]{4,3,2,1,0:T(8,128)(2,1)} %param.14) | copy-start | bytes 1179652
  7.2 408.5 %reduce-scatter.7.cloned.1.call-start = ((), (), s32[]{:S(2)}) async-start(), calls=%async_computation.2 | async-start | bytes 835584
  8.3 13.8 %copy-start.18 = (bf16[96,64]{0,1:T(8,128)(2,1)S(1)}, bf16[96,64]{0,1:T(8,128)(2,1)}, u32[]{:S(2)}) copy-start(bf16[96,64]{0,1:T(8,128)(2,1)} %param.18) | copy-start | bytes 36868
  9.4 53.1 %copy-start.17 = (bf16[64,192]{1,0:T(8,128)(2,1)S(1)}, bf16[64,192]{1,0:T(8,128)(2,1)}, u32[]{:S(2)}) copy-start(bf16[64,192]{1,0:T(8,128)(2,1)} %param.19) | copy-start | bytes 73732
  10.4 93.2 %collective-permute-start = (bf16[2,1,2,32,1536]{4,3,2,1,0:T(8,128)(2,1)}, bf16[2,1,2,32,1536]{4,3,2,1,0:T(8,128)(2,1)S(1)}, u32[]{:S(2)}, u32[]{:S(2)}) collective-permute-start(bf16[2,1,2,32,1536]{4,3,2,1,0:T(8,128)(2,1)} %get-tuple-element.10), channel_id=1, source_target_pairs={{0,128},{128,256},{256,384},{1,129},{129,257},{257,385},{2,130},{1... | collective-permute-start | bytes 1179656 | tf_op jit(solution)/shard_map/ppermute | solution.py:25
  15.8 87.8 %collective-permute-start.1 = (bf16[2,1,2,32,1536]{4,3,2,1,0:T(8,128)(2,1)}, bf16[2,1,2,32,1536]{4,3,2,1,0:T(8,128)(2,1)S(1)}, u32[]{:S(2)}, u32[]{:S(2)}) collective-permute-start(bf16[2,1,2,32,1536]{4,3,2,1,0:T(8,128)(2,1)} %get-tuple-element.11), channel_id=1, source_target_pairs={{128,0},{256,128},{384,256},{129,1},{257,129},{385,257},{130,2},{2... | collective-permute-start | bytes 1179656 | tf_op jit(solution)/shard_map/ppermute | solution.py:27
  62.2 38.6 %copy-start.10 = (f32[1,2,2,2048]{3,2,1,0:T(2,128)S(1)}, f32[1,2,2,2048]{3,2,1,0:T(2,128)}, u32[]{:S(2)}) copy-start(f32[1,2,2,2048]{3,2,1,0:T(2,128)} %param.24) | copy-start | bytes 98308
  62.2 39.4 %copy-start.9 = (f32[1,2,2,2048]{3,2,1,0:T(2,128)S(1)}, f32[1,2,2,2048]{3,2,1,0:T(2,128)}, u32[]{:S(2)}) copy-start(f32[1,2,2,2048]{3,2,1,0:T(2,128)} %param.25) | copy-start | bytes 98308
  99.4 51.5 %copy-start.1 = (bf16[3072,64]{0,1:T(8,128)(2,1)}, bf16[3072,64]{0,1:T(8,128)(2,1)S(1)}, u32[]{:S(2)}) copy-start(bf16[3072,64]{0,1:T(8,128)(2,1)S(1)} %reshape.312) | copy-start | bytes 1179652
  103.8 5.5 copy-start.22
  103.8 5.5 copy-start.16
  103.9 23.4 %collective-permute-start.2 = (bf16[2,4,1,32,1536]{4,3,2,1,0:T(8,128)(2,1)S(1)}, bf16[2,4,1,32,1536]{4,3,2,1,0:T(8,128)(2,1)S(1)}, u32[]{:S(2)}, u32[]{:S(2)}) collective-permute-start(bf16[2,4,1,32,1536]{4,3,2,1,0:T(8,128)(2,1)S(1)} %get-tuple-element.8), channel_id=1, source_target_pairs={{0,8},{8,16},{16,24},{24,32},{32,40},{40,48},{48,56},{56,64},{64,7... | collective-permute-start | bytes 2359304 | tf_op jit(solution)/shard_map/ppermute | solution.py:25
  107.9 24.8 %collective-permute-start.3 = (bf16[2,4,1,32,1536]{4,3,2,1,0:T(8,128)(2,1)S(1)}, bf16[2,4,1,32,1536]{4,3,2,1,0:T(8,128)(2,1)S(1)}, u32[]{:S(2)}, u32[]{:S(2)}) collective-permute-start(bf16[2,4,1,32,1536]{4,3,2,1,0:T(8,128)(2,1)S(1)} %get-tuple-element.9), channel_id=1, source_target_pairs={{8,0},{16,8},{24,16},{32,24},{40,32},{48,40},{56,48},{64,56},{72,6... | collective-permute-start | bytes 2359304 | tf_op jit(solution)/shard_map/ppermute | solution.py:27
  109.9 41.0 %copy-start.12 = (f32[1,1,3072]{2,0,1:T(1,128)}, f32[1,1,3072]{2,0,1:T(1,128)S(1)}, u32[]{:S(2)}) copy-start(f32[1,1,3072]{2,0,1:T(1,128)S(1)} %get-tuple-element.13) | copy-start | bytes 36868
  109.9 41.9 %copy-start.14 = (f32[1,1,3072]{2,0,1:T(1,128)}, f32[1,1,3072]{2,0,1:T(1,128)S(1)}, u32[]{:S(2)}) copy-start(f32[1,1,3072]{2,0,1:T(1,128)S(1)} %get-tuple-element.12) | copy-start | bytes 36868
  138.5 2.1 copy-start.6
  138.5 2.1 copy-start.8
  146.9 4.0 copy-start.5
  150.7 0.8 copy-start.3
  150.9 0.9 copy-start.19
  150.9 0.9 copy-start.23
  151.5 156.3 %copy-start.20 = (f32[128]{0:T(128)}, f32[128]{0:T(128)S(1)}, u32[]{:S(2)}) copy-start(f32[128]{0:T(128)S(1)} %broadcast_multiply_fusion.2) | copy-start | bytes 1540
  151.8 155.2 %copy-start.11 = (f32[128,64]{0,1:T(8,128)S(1)}, f32[128,64]{0,1:T(8,128)}, u32[]{:S(2)}) copy-start(f32[128,64]{0,1:T(8,128)} %copy.35) | copy-start | bytes 98308
  151.8 156.0 %copy-start.21 = (f32[128]{0:T(128)}, f32[128]{0:T(128)S(1)}, u32[]{:S(2)}) copy-start(f32[128]{0:T(128)S(1)} %add_rsqrt_fusion) | copy-start | bytes 1540
  307.0 0.8 copy-start.15
  307.8 0.8 copy-start.13
  308.7 1.3 copy-start.2
  310.4 1.0 copy-start.4
  313.3 197.6 %reduce-scatter.9.cloned.1.call-start = ((), (), s32[]{:S(2)}) async-start(), calls=%async_computation.3 | async-start | bytes 1671168
  315.9 416.3 %all-reduce.3.cloned.1.call-start = ((), (), s32[]{:S(2)}) async-start(), calls=%async_computation.4 | async-start | bytes 196608 | tf_op jit(solution)/shard_map/psum | solution.py:238
Sparse Core Ops, SparseCore 0:
  313.5 102.1 reduce-scatter.6
  419.8 91.1 reduce-scatter.8
  514.5 217.6 all-reduce.2
where the time goes:
time: 742 us
  waiting for transfers between devices  436 us (59%)
  blocking collectives  229 us (31%)
  local copies, waits for them, and re-layouts  23.7 us (3%)
  between operations  16.3 us (2%)
  matrix products  15.7 us (2%)
  starting transfers between devices  15.5 us (2%)
    psum x1, waiting for transfers between devices, body(): share_a, share_b = lax.psum((shares[0], shares[1]), ('tm', 'group'))  220 us
    unnamed x5, waiting for transfers between devices  194 us
    psum x1, blocking collectives, coefficient(): fit_total = lax.psum(partial_value, ('tm', 'height'))  153 us
    all_gather x1, blocking collectives, body(): lax.all_gather(adapter_down_factor, 'height', axis=0, tiled=True)  39.8 us
    all_gather x1, blocking collectives, body(): lax.all_gather(adapter_up_factor, 'height', axis=1, tiled=True)  36.1 us
    ppermute x2, waiting for transfers between devices, padded(): lax.ppermute(tail, axis, [(i, (i + 1) % count) for i in range(ends)])  17.4 us
  transfers between devices with their start and end apart: 7, of which 5 were waited for; matrix products, arithmetic and copies ran while one was open for 1% of the time, Pallas kernels for 0%

commit v1 on v0

v1 whole, which is shorter than its diff:
```python
import functools
import math

import jax
import jax.numpy as jnp
from jax import lax
from jax.experimental import pallas as pl
from jax.experimental.pallas import tpu as pltpu
from jax.sharding import PartitionSpec as P

TILE_W = 8
COLS = 32
HEAD = 128
RANK = 64
LAT = 64
SAMPLER_STEP = -0.5
CLIP_RANGE = 0.2
NORM_EPS = 1e-06
HALF_LOG_TAU = 0.5 * math.log(2.0 * math.pi)
DOWN_SHARD = 96
UP_SHARD = 192
PIECE = 144
HALF = 80
FAR = 32768.0
F32 = jnp.float32
BF16 = jnp.bfloat16
MESH = pl.DeviceIdType.MESH


def dot(a, b, ca, cb):
    return lax.dot_general(a, b, (((ca,), (cb,)), ((), ())), preferred_element_type=F32)


def kernel(
    dims,
    q_hbm, k_hbm, v_hbm, win, a_t, b_own, st_hbm, mod, w_hbm, bias, lat, nxt, slp, adv,
    out,
    q, kv, st, w_t, gath, a_full, b_full, att, hid, gn, pack, mate, chip, got, ysum, final,
    d2, dn, part_tm, part_h, load_sem, halo_send, halo_recv, g_send, g_recv, s_send, s_recv,
    r_send, r_recv,
):
    n_tm, n_h, n_g, n_z, heads, group_heads = dims
    width = heads * HEAD
    model = st.shape[-1]
    n_x = n_h // n_z
    tm, me_h, me_g = lax.axis_index("tm"), lax.axis_index("height"), lax.axis_index("group")
    core, z_lo = lax.rem(tm, 2), tm // 2
    me_x, me_z = me_h // n_z, lax.rem(me_h, n_z)
    half_h = n_h // 2

    loads = [
        pltpu.make_async_copy(k_hbm.at[0], kv.at[0, 1:3, 1:3], load_sem.at[0]),
        pltpu.make_async_copy(v_hbm.at[0], kv.at[1, 1:3, 1:3], load_sem.at[1]),
        pltpu.make_async_copy(q_hbm.at[0], q, load_sem.at[2]),
        pltpu.make_async_copy(st_hbm.at[0], st, load_sem.at[3]),
        pltpu.make_async_copy(w_hbm, w_t, load_sem.at[4]),
    ]
    for load in loads:
        load.start()

    barrier = pltpu.get_barrier_semaphore()
    plane = 2 * n_h

    def greet_plane(i, _):
        at = lax.rem(me_h * 2 + z_lo + i, plane)
        pl.semaphore_signal(
            barrier, inc=1, device_id=(2 * lax.rem(at, 2) + core, at // 2, me_g), device_id_type=MESH
        )
        return 0

    lax.fori_loop(1, plane, greet_plane, 0)

    def greet_group(i, _):
        pl.semaphore_signal(
            barrier, inc=1, device_id=(tm, me_h, lax.rem(me_g + i, n_g)), device_id_type=MESH
        )
        return 0

    lax.fori_loop(1, n_g, greet_group, 0)
    for zl in range(2):
        pl.semaphore_signal(
            barrier, inc=1, device_id=(2 * zl + 1 - core, me_h, me_g), device_id_type=MESH
        )

    lane = lax.broadcasted_iota(jnp.int32, (1, 128), 1)
    left = lane < 64
    unit_row = lax.broadcasted_iota(jnp.int32, (64, 128), 0)
    unit_lane = lax.broadcasted_iota(jnp.int32, (64, 128), 1)
    twice = (lax.rem(unit_lane, 64) == unit_row).astype(F32).astype(BF16)
    b_rows = dot(b_own[...], twice, 0, 0)
    a_rows = dot(a_t[...], twice, 0, 0)
    own_rows = jnp.concatenate(
        [jnp.where(left, b_rows[0:96], b_rows[96:192]), jnp.where(left, a_rows[0:48], a_rows[48:96])],
        axis=0,
    ).astype(BF16)

    @pl.when(core == 0)
    def _():
        gath[me_h, 0:HALF, :] = own_rows[0:HALF]

    @pl.when(core == 1)
    def _():
        gath[me_h, HALF:PIECE, :] = own_rows[HALF:PIECE]

    first_tm, last_tm = tm == 0, tm == n_tm - 1
    first_h, last_h = me_h == 0, me_h == n_h - 1

    @pl.when(first_tm)
    def _():
        kv[:, 0:1] = jnp.zeros((2, 1, 4, COLS, width), BF16)

    @pl.when(last_tm)
    def _():
        kv[:, 3:4] = jnp.zeros((2, 1, 4, COLS, width), BF16)

    @pl.when(first_h)
    def _():
        kv[:, :, 0:1] = jnp.zeros((2, 4, 1, COLS, width), BF16)

    @pl.when(last_h)
    def _():
        kv[:, :, 3:4] = jnp.zeros((2, 4, 1, COLS, width), BF16)

    loads[0].wait()
    loads[1].wait()
    pl.semaphore_wait(barrier, plane - 1 + n_g - 1 + 2)

    n_parts = heads // group_heads
    ahead_h = (tm, jnp.minimum(me_h + 1, n_h - 1), me_g)
    back_h = (tm, jnp.maximum(me_h - 1, 0), me_g)
    ahead_tm = (jnp.minimum(tm + 1, n_tm - 1), me_h, me_g)
    back_tm = (jnp.maximum(tm - 1, 0), me_h, me_g)

    def halo(part, way):
        cols = pl.ds(part * group_heads * HEAD, group_heads * HEAD)
        src, dst, to = {
            0: (kv.at[:, 1:3, 2, :, cols], kv.at[:, 1:3, 0, :, cols], ahead_h),
            1: (kv.at[:, 1:3, 1, :, cols], kv.at[:, 1:3, 3, :, cols], back_h),
            2: (kv.at[:, 2, 1:3, :, cols], kv.at[:, 0, 1:3, :, cols], ahead_tm),
            3: (kv.at[:, 1, 1:3, :, cols], kv.at[:, 3, 1:3, :, cols], back_tm),
            4: (kv.at[:, 2, 0, :, cols], kv.at[:, 0, 0, :, cols], ahead_tm),
            5: (kv.at[:, 1, 0, :, cols], kv.at[:, 3, 0, :, cols], back_tm),
            6: (kv.at[:, 2, 3, :, cols], kv.at[:, 0, 3, :, cols], ahead_tm),
            7: (kv.at[:, 1, 3, :, cols], kv.at[:, 3, 3, :, cols], back_tm),
        }[way]
        return pltpu.make_async_remote_copy(
            src_ref=src, dst_ref=dst, send_sem=halo_send.at[part, way], recv_sem=halo_recv.at[part, way],
            device_id=to, device_id_type=MESH,
        )

    not_first_tm, not_last_tm = tm > 0, tm < n_tm - 1
    not_first_h, not_last_h = me_h > 0, me_h < n_h - 1
    sends = {
        0: not_last_h, 1: not_first_h, 2: not_last_tm, 3: not_first_tm,
        4: not_first_h & not_last_tm, 5: not_first_h & not_first_tm,
        6: not_last_h & not_last_tm, 7: not_last_h & not_first_tm,
    }
    receives = {
        0: not_first_h, 1: not_last_h, 2: not_first_tm, 3: not_last_tm,
        4: not_first_h & not_first_tm, 5: not_first_h & not_last_tm,
        6: not_last_h & not_first_tm, 7: not_last_h & not_last_tm,
    }

    def when_each(table, ways, part, act):
        for way in ways:
            @pl.when(table[way])
            def _(way=way):
                act(halo(part, way))

    my_rows = pl.ds(pl.multiple_of(core * HALF, 16), HALF)

    def gather_z(i):
        src = gath.at[me_h, my_rows]
        to = (tm, me_x * n_z + lax.rem(me_z + i, n_z), me_g)
        return pltpu.make_async_remote_copy(
            src_ref=src, dst_ref=src, send_sem=g_send.at[i], recv_sem=g_recv.at[0],
            device_id=to, device_id_type=MESH,
        )

    def gather_x(i):
        src = gath.at[pl.ds(me_x * n_z, n_z), my_rows]
        to = (tm, lax.rem(me_x + i, n_x) * n_z + me_z, me_g)
        return pltpu.make_async_remote_copy(
            src_ref=src, dst_ref=src, send_sem=g_send.at[n_z + i], recv_sem=g_recv.at[1],
            device_id=to, device_id_type=MESH,
        )

    def gather_core():
        src = gath.at[:, my_rows]
        return pltpu.make_async_remote_copy(
            src_ref=src, dst_ref=src, send_sem=g_send.at[0], recv_sem=g_recv.at[2],
            device_id=(2 * z_lo + 1 - core, me_h, me_g), device_id_type=MESH,
        )

    for part in range(n_parts):
        when_each(sends, (0, 1, 2, 3), part, lambda copy: copy.start())
        if part == 0:
            for i in range(1, n_z):
                gather_z(i).start()

    tokens = 4 * COLS
    q_at = lax.broadcasted_iota(jnp.int32, (tokens, 128), 0)
    feature = lax.broadcasted_iota(jnp.int32, (tokens, 128), 1)
    q_frame, q_row, q_tile = q_at // 64, lax.rem(q_at // 32, 2), lax.rem(q_at, 32) // TILE_W
    frame_at = tm * 2 - 1 + feature
    row_at = me_h * 2 - 1 + (feature - 4)
    gap_frame = jnp.where(
        (frame_at >= 0) & (frame_at < 2 * n_tm), jnp.abs(q_frame + 1 - feature), 99
    )
    gap_row = jnp.where(
        (row_at >= 0) & (row_at < 2 * n_h), jnp.abs(q_row + 1 - (feature - 4)), 99
    )
    gap_tile = jnp.abs(q_tile - (feature - 8))
    gap = jnp.where(
        feature < 4, gap_frame,
        jnp.where(feature < 8, gap_row, jnp.where(feature < 12, gap_tile, -1)),
    )
    k_at = lax.broadcasted_iota(jnp.int32, (512, 128), 0)
    k_feature = lax.broadcasted_iota(jnp.int32, (512, 128), 1)
    k_one_hot = (
        (k_feature == k_at // 128)
        | (k_feature == 4 + lax.rem(k_at // 32, 4))
        | (k_feature == 8 + lax.rem(k_at, 32) // TILE_W)
    ).astype(F32).astype(BF16)
    ones = jnp.ones((512, 128), BF16)
    factor = HEAD**-0.5 * math.log2(math.e)

    def attend(part):
        for head in range(part * group_heads, (part + 1) * group_heads):
            cols = pl.ds(head * HEAD, HEAD)
            reach = jnp.where(
                lane < 4, win[0, head], jnp.where(lane < 8, win[1, head], win[2, head])
            )
            penalty = jnp.where(gap > reach, -FAR, 0.0).astype(BF16)
            query = jnp.concatenate([q[:, :, :, cols].reshape(tokens, HEAD), penalty], axis=1)
            key = jnp.concatenate([kv[0, :, :, :, cols].reshape(512, HEAD), k_one_hot], axis=1)
            scores = dot(query, key, 1, 1)
            top = jnp.max(scores, axis=1, keepdims=True)
            terms = jnp.exp2((scores - top) * factor).astype(BF16)
            value = jnp.concatenate([kv[1, :, :, :, cols].reshape(512, HEAD), ones], axis=1)
            mixed = dot(terms, value, 1, 0)
            att[:, cols] = (mixed[:, :HEAD] / mixed[:, HEAD:]).astype(BF16)

    loads[2].wait()
    for part in range(n_parts):
        when_each(receives, (0, 1), part, lambda copy: copy.wait_recv())
        when_each(sends, (4, 5, 6, 7), part, lambda copy: copy.start())
        if part == 0:
            for i in range(1, n_z):
                gather_z(i).wait_send()
            taken = gath.at[pl.ds(0, n_z - 1), my_rows]
            pltpu.make_async_copy(taken, taken, g_recv.at[0]).wait()
            for i in range(1, n_x):
                gather_x(i).start()
        if part == 1:
            for i in range(1, n_x):
                gather_x(i).wait_send()
            taken = gath.at[pl.ds(0, (n_x - 1) * n_z), my_rows]
            pltpu.make_async_copy(taken, taken, g_recv.at[1]).wait()
            gather_core().start()
        if part >= 1:
            when_each(receives, (2, 3, 4, 5, 6, 7), part - 1, lambda copy: copy.wait_recv())
            attend(part - 1)
        if part == min(2, n_parts - 1):
            gather_core().wait()
            for h in range(n_h):
                both = gath[h, 0:96, :]
                b_full[h * 192 : h * 192 + 96, :] = both
                b_full[h * 192 + 96 : h * 192 + 192, 0:64] = both[:, 64:128]
                both = gath[h, 96:144, :]
                a_full[h * 96 : h * 96 + 48, :] = both
                a_full[h * 96 + 48 : h * 96 + 96, 0:64] = both[:, 64:128]
            for f in range(2):
                for j in range(16):
                    cols = pl.ds(j * 128, 128)
                    d2[pl.ds(f * 32 + 2 * j, 2), :] = nxt[0, f, :, cols] - lat[0, f, :, cols]
            for f in range(2):
                for r in range(2):
                    pair = d2[pl.ds(f * 32 + r, 16, stride=2), :]
                    dn[pl.ds(f * 64 + r * 32, 16, stride=2), :] = pair
                    dn[pl.ds(f * 64 + r * 32 + 1, 16, stride=2), :] = pltpu.roll(pair, 64, 1)
            loads[3].wait()
            loads[4].wait()
    when_each(receives, (2, 3, 4, 5, 6, 7), n_parts - 1, lambda copy: copy.wait_recv())
    attend(n_parts - 1)

    step = 2 * UP_SHARD
    chunks = [pl.ds(i * step, step) for i in range(model // step)]

    def fold(x):
        total = x[:, 0:128]
        for i in range(1, x.shape[1] // 128):
            total = total + x[:, i * 128 : (i + 1) * 128]
        return total

    def mean(total):
        return jnp.sum(total, axis=1, keepdims=True) * (1.0 / model)

    low = dot(att[...], a_full[:, 0:64], 1, 0).astype(BF16)
    total = jnp.zeros((tokens, 128), F32)
    for cols in chunks:
        update = dot(low, b_full[cols, 0:64], 1, 1)
        rows = st[:, :, :, cols].reshape(tokens, step).astype(F32)
        hidden = rows + mod[0, :, cols] * update
        hid[:, cols] = hidden
        total = total + fold(hidden)
    centre = mean(total)
    total = jnp.zeros((tokens, 128), F32)
    for cols in chunks:
        apart = hid[:, cols] - centre
        total = total + fold(apart * apart)
    inverse = lax.rsqrt(mean(total) + NORM_EPS)
    velocity = jnp.zeros((tokens, LAT), F32)
    for cols in chunks:
        normal = (hid[:, cols] - centre) * inverse
        hid[:, cols] = normal
        normed = (normal * (1.0 + mod[2, :, cols]) + mod[1, :, cols]).astype(BF16)
        velocity = velocity + dot(normed, w_t[:, cols], 1, 1)
    residue = dn[:, 0:64] - SAMPLER_STEP * (velocity + bias[...])

    square = jnp.sum(jnp.sum(residue * residue, axis=0, keepdims=True), axis=1, keepdims=True)
    part_tm[tm] = jnp.broadcast_to(square, (8, 128))

    def sum_tm(i):
        return pltpu.make_async_remote_copy(
            src_ref=part_tm.at[tm], dst_ref=part_tm.at[tm], send_sem=s_send.at[i], recv_sem=s_recv.at[0],
            device_id=(lax.rem(tm + i, n_tm), me_h, me_g), device_id_type=MESH,
        )

    def sum_h(i):
        return pltpu.make_async_remote_copy(
            src_ref=part_h.at[me_h], dst_ref=part_h.at[me_h], send_sem=s_send.at[n_tm + i], recv_sem=s_recv.at[1],
            device_id=(tm, lax.rem(me_h + i, n_h), me_g), device_id_type=MESH,
        )

    for i in range(1, n_tm):
        sum_tm(i).start()

    g_velocity = (SAMPLER_STEP * residue).astype(BF16)
    total = jnp.zeros((tokens, 128), F32)
    total_n = jnp.zeros((tokens, 128), F32)
    for cols in chunks:
        g_normal = dot(g_velocity, w_t[:, cols], 1, 0) * (1.0 + mod[2, :, cols])
        gn[:, cols] = g_normal
        total = total + fold(g_normal)
        total_n = total_n + fold(g_normal * hid[:, cols])
    mean_g, mean_gn = mean(total), mean(total_n)

    for i in range(1, n_tm):
        sum_tm(i).wait_send()
    pltpu.make_async_copy(part_tm.at[0 : n_tm - 1], part_tm.at[0 : n_tm - 1], s_recv.at[0]).wait()
    square = part_tm[0]
    for i in range(1, n_tm):
        square = square + part_tm[i]
    part_h[me_h] = square
    for i in range(1, n_h):
        sum_h(i).start()

    g_low = jnp.zeros((tokens, RANK), F32)
    for pair, cols in enumerate(chunks):
        g_out = mod[0, :, cols] * (inverse * (gn[:, cols] - mean_g - hid[:, cols] * mean_gn))
        g_out = g_out.astype(BF16)
        g_low = g_low + dot(g_out, b_full[cols, 0:64], 1, 0)
        up = dot(low, g_out, 0, 0)
        pack[pair, 0, 0:64, :] = up[:, 0:128].astype(BF16)
        pack[pair, 1, 0:64, :] = up[:, 256:384].astype(BF16)
        shared = up[:, 128:256]
        turned = pltpu.roll(shared, 64, 1)
        pack[pair, 0, 64:96, :] = jnp.where(left, shared[0:32], turned[32:64]).astype(BF16)
        pack[pair, 1, 64:96, :] = jnp.where(left, turned[0:32], shared[32:64]).astype(BF16)

    partner = (2 * z_lo + 1 - core, me_h, me_g)

    def to_mate(i):
        rows = (pl.ds(0, 96), pl.ds(96, 48))[i]
        return pltpu.make_async_remote_copy(
            src_ref=pack.at[:, 1 - core, rows], dst_ref=mate.at[:, rows],
            send_sem=r_send.at[i], recv_sem=r_recv.at[i], device_id=partner, device_id_type=MESH,
        )

    to_mate(0).start()
    g_low_twice = jnp.concatenate([g_low, g_low], axis=1).astype(BF16)
    for pair in range(half_h):
        down = dot(att[:, pl.ds(pair * 192, 192)], g_low_twice, 0, 0)
        for i in range(2):
            top, low_end = down[i * 96 : i * 96 + 48], down[i * 96 + 48 : i * 96 + 96]
            pack[pair, i, 96:144, :] = jnp.where(left, top, low_end).astype(BF16)
    to_mate(1).start()

    for i in range(2):
        to_mate(i).wait()
        rows = (pl.ds(0, 96), pl.ds(96, 48))[i]
        for j in range(half_h):
            chip[j, rows, :] = (
                pack[j, core, rows, :].astype(F32) + mate[j, rows, :].astype(F32)
            ).astype(BF16)

    takes = lax.rem(me_h, 2) == core
    slot = me_h * 2 + z_lo
    part_rows = (pl.ds(0, HALF), pl.ds(HALF, PIECE - HALF))

    def to_owner(i, zl):
        j = lax.rem(me_h // 2 + i, half_h)
        size = (HALF, PIECE - HALF)[zl]
        return pltpu.make_async_remote_copy(
            src_ref=chip.at[j, part_rows[zl]], dst_ref=got.at[slot, pl.ds(0, size)],
            send_sem=r_send.at[2 + 2 * i + zl], recv_sem=r_recv.at[2],
            device_id=(2 * zl + core, 2 * j + core, me_g), device_id_type=MESH,
        )

    for i in range(half_h):
        for zl in range(2):
            if i == 0:
                own = takes & (z_lo == zl)

                @pl.when(own)
                def _(zl=zl):
                    size = (HALF, PIECE - HALF)[zl]
                    got[slot, 0:size, :] = chip[me_h // 2, part_rows[zl], :]

                @pl.when(jnp.logical_not(own))
                def _(zl=zl):
                    to_owner(0, zl).start()
            else:
                to_owner(i, zl).start()

    for i in range(1, n_h):
        sum_h(i).wait_send()
    pltpu.make_async_copy(part_h.at[0 : n_h - 1], part_h.at[0 : n_h - 1], s_recv.at[1]).wait()
    square = part_h[0]
    for i in range(1, n_h):
        square = square + part_h[i]
    square = square[0:1, :]
    count = 4 * COLS * LAT * n_tm * n_h
    logp = -square / (2.0 * count) - HALF_LOG_TAU
    gain = adv[0]
    ratio = jnp.exp(logp - slp[0])
    low_end, high_end = 1.0 - CLIP_RANGE, 1.0 + CLIP_RANGE
    plain = -gain * ratio
    cut = -gain * jnp.clip(ratio, low_end, high_end)
    inside = jnp.where(
        (ratio > low_end) & (ratio < high_end), 1.0,
        jnp.where((ratio == low_end) | (ratio == high_end), 0.5, 0.0),
    )
    weight = jnp.where(plain > cut, 1.0, jnp.where(plain == cut, 0.5 + 0.5 * inside, inside))
    slope = weight * plain * (1.0 / n_g)

    def to_group(i):
        return pltpu.make_async_remote_copy(
            src_ref=ysum.at[me_g], dst_ref=ysum.at[me_g], send_sem=r_send.at[2 + n_h + i], recv_sem=r_recv.at[3],
            device_id=(tm, me_h, lax.rem(me_g + i, n_g)), device_id_type=MESH,
        )

    def to_tm(i):
        there = lax.rem(tm + i, n_tm)
        return pltpu.make_async_remote_copy(
            src_ref=final.at[z_lo], dst_ref=final.at[z_lo], send_sem=r_send.at[2 + n_h + n_g + i],
            recv_sem=r_recv.at[4 + z_lo], device_id=(there, me_h, me_g), device_id_type=MESH,
        )

    @pl.when(takes)
    def _():
        for zl in range(2):
            @pl.when(z_lo == zl)
            def _(zl=zl):
                arrived = got.at[0 : plane - 1, pl.ds(0, (HALF, PIECE - HALF)[zl])]
                pltpu.make_async_copy(arrived, arrived, r_recv.at[2]).wait()
        share = got[0].astype(F32)
        for i in range(1, plane):
            share = share + got[i].astype(F32)
        ysum[me_g] = (share * slope).astype(BF16)
        for i in range(1, n_g):
            to_group(i).start()
        pltpu.make_async_copy(ysum.at[0 : n_g - 1], ysum.at[0 : n_g - 1], r_recv.at[3]).wait()
        share = ysum[0].astype(F32)
        for i in range(1, n_g):
            share = share + ysum[i].astype(F32)
        final[z_lo] = share
        for i in range(1, n_tm):
            to_tm(i).start()
        other = 1 - z_lo
        pltpu.make_async_copy(final.at[other], final.at[other], r_recv.at[4 + other]).wait()
        for i in range(1, n_g):
            to_group(i).wait_send()
        for i in range(1, n_tm):
            to_tm(i).wait_send()

    @pl.when(jnp.logical_not(takes))
    def _():
        for zl in range(2):
            pltpu.make_async_copy(final.at[zl], final.at[zl], r_recv.at[4 + zl]).wait()

    out[0:HALF, :] = final[0]
    out[HALF:PIECE, :] = final[1, 0 : PIECE - HALF, :]

    for part in range(n_parts):
        when_each(sends, range(8), part, lambda copy: copy.wait_send())
    for i in range(half_h):
        for zl in range(2):
            if i == 0:
                @pl.when(jnp.logical_not(takes & (z_lo == zl)))
                def _(zl=zl):
                    to_owner(0, zl).wait_send()
            else:
                to_owner(i, zl).wait_send()


def unpack_kernel(packed, down_t, up):
    odd = lax.rem(lax.axis_index("height"), 2) == 1
    full = packed[0:64, :]
    rest = packed[64:96, :]
    narrow = jnp.concatenate([rest[:, 0:64], rest[:, 64:128]], axis=0)

    @pl.when(odd)
    def _():
        up[...] = jnp.concatenate([narrow, full], axis=1)

    @pl.when(jnp.logical_not(odd))
    def _():
        up[...] = jnp.concatenate([full, narrow], axis=1)

    down = packed[96:144, :]
    down = jnp.concatenate([down[:, 0:64], down[:, 64:128]], axis=0)
    down_t[...] = down.T


def body(
    queries, keys, values, window, adapter_down_factor, adapter_up_factor, stream, modulation,
    closing_weight, closing_bias, latent, next_latent_sample, sampling_log_probability, advantage,
):
    heads = window.shape[0]
    width = heads * HEAD
    model = stream.shape[-1]
    n_tm, n_h, n_g = lax.axis_size("tm"), lax.axis_size("height"), lax.axis_size("group")
    n_z = 4 if n_h == 16 else 2
    group_heads = 3 if heads % 3 == 0 and heads > 3 else 1
    dims = (n_tm, n_h, n_g, n_z, heads, group_heads)
    n_parts = heads // group_heads
    tokens = 4 * COLS
    vmem = pl.BlockSpec(memory_space=pltpu.VMEM)
    smem = pl.BlockSpec(memory_space=pltpu.SMEM)
    hbm = pl.BlockSpec(memory_space=pl.ANY)
    dma = pltpu.SemaphoreType.DMA
    packed = pl.pallas_call(
        functools.partial(kernel, dims),
        out_shape=jax.ShapeDtypeStruct((PIECE, 128), F32),
        in_specs=[hbm, hbm, hbm, smem, vmem, vmem, hbm, vmem, hbm, vmem, vmem, vmem, smem, smem],
        out_specs=vmem,
        scratch_shapes=[
            pltpu.VMEM((2, 2, COLS, width), BF16),
            pltpu.VMEM((2, 4, 4, COLS, width), BF16),
            pltpu.VMEM((2, 2, COLS, model), BF16),
            pltpu.VMEM((LAT, model), BF16),
            pltpu.VMEM((n_h, 2 * HALF, 128), BF16),
            pltpu.VMEM((width, 128), BF16),
            pltpu.VMEM((model, 128), BF16),
            pltpu.VMEM((tokens, width), BF16),
            pltpu.VMEM((tokens, model), F32),
            pltpu.VMEM((tokens, model), F32),
            pltpu.VMEM((n_h // 2, 2, PIECE, 128), BF16),
            pltpu.VMEM((n_h // 2, PIECE, 128), BF16),
            pltpu.VMEM((n_h // 2, PIECE, 128), BF16),
            pltpu.VMEM((2 * n_h, HALF, 128), BF16),
            pltpu.VMEM((n_g, HALF, 128), BF16),
            pltpu.VMEM((2, HALF, 128), F32),
            pltpu.VMEM((64, 128), F32),
            pltpu.VMEM((128, 128), F32),
            pltpu.VMEM((n_tm, 8, 128), F32),
            pltpu.VMEM((n_h, 8, 128), F32),
            dma((5,)),
            dma((n_parts, 8)),
            dma((n_parts, 8)),
            dma((n_h,)),
            dma((3,)),
            dma((n_tm + n_h,)),
            dma((2,)),
            dma((2 + n_h + n_g + n_tm,)),
            dma((6,)),
        ],
        compiler_params=pltpu.CompilerParams(
            collective_id=0, has_side_effects=True, vmem_limit_bytes=48 * 1024 * 1024
        ),
        name="step",
    )(
        queries, keys, values, window.T, adapter_down_factor.T, adapter_up_factor, stream,
        modulation.transpose(1, 0, 2), closing_weight.T, closing_bias.reshape(1, LAT), latent,
        next_latent_sample, sampling_log_probability, advantage,
    )
    down_t, up = pl.pallas_call(
        unpack_kernel,
        out_shape=(
            jax.ShapeDtypeStruct((RANK, DOWN_SHARD), F32),
            jax.ShapeDtypeStruct((RANK, UP_SHARD), F32),
        ),
        in_specs=[vmem],
        out_specs=(vmem, vmem),
        name="unpack",
    )(packed)
    return (down_t.T, up)


def solution(mesh):
    return jax.shard_map(
        body,
        mesh=mesh,
        in_specs=(
            P("group", "tm", "height", None, None),
            P("group", "tm", "height", None, None),
            P("group", "tm", "height", None, None),
            P(),
            P("height", None),
            P(None, "height"),
            P("group", "tm", "height", None, None),
            P("group", None, None),
            P(),
            P(),
            P("group", "tm", "height", None),
            P("group", "tm", "height", None),
            P("group"),
            P("group"),
        ),
        out_specs=(P("height", None), P(None, "height")),
        check_vma=False,
    )
```

time: 742 us -> 91.4 us (0.12)
  waiting for transfers between devices: 436 us -> 0 us
  blocking collectives: 229 us -> 0 us
  Pallas kernels: 0 us -> 78.6 us
  matrix products: 15.7 us -> 0 us
  starting transfers between devices: 15.5 us -> 0 us
  between operations: 16.3 us -> 1.97 us
  local copies, waits for them, and re-layouts: 23.7 us -> 10.2 us
    psum x1 -> x0, waiting for transfers between devices: 220 us -> none  [body(): share_a, share_b = lax.psum((shares[0], shares[1]), ('tm', 'group'))]
    unnamed x5 -> x0, waiting for transfers between devices: 194 us -> none
    psum x1 -> x0, blocking collectives: 153 us -> none  [coefficient(): fit_total = lax.psum(partial_value, ('tm', 'height'))]
    pallas_call x0 -> x2, Pallas kernels: none -> 78.6 us  [the longest x1 76.9 us: body(): pl.pallas_call(functools.partial(kernel, dims), out_shape=jax.ShapeDtypeS...]
    all_gather x2 -> x0, blocking collectives: 76 us -> none  [the longest x1 39.8 us: body(): lax.all_gather(adapter_down_factor, 'height', axis=0, tiled=True)]
    ppermute x4 -> x0, waiting for transfers between devices: 22.8 us -> none  [the longest x2 17.4 us: padded(): lax.ppermute(tail, axis, [(i, (i + 1) % count) for i in range(ends)])]
    ppermute x4 -> x0, starting transfers between devices: 15.4 us -> none  [the longest x2 9.41 us: padded(): lax.ppermute(tail, axis, [(i, (i + 1) % count) for i in range(ends)])]
    dot_general x16 -> x0, matrix products: 9.31 us -> none  [the longest x1 3.73 us: attend(): jnp.einsum('hqk,khd->qhd', weights, value_block, preferred_element_type=j...]
  transfers between devices with their start and end apart: 7 -> 0, of which waited for: 5 -> 0; matrix products, arithmetic and copies ran while one was open for 1% -> 0% of each run, Pallas kernels for 0% -> 0%
where the time goes in v1:
time: 91.4 us; the launch traced here: 90.7 us
  Pallas kernels  78.6 us (86%)
  local copies, waits for them, and re-layouts  10.2 us (11%)
  between operations  1.97 us (2%)
    pallas_call x1, Pallas kernels, body(): pl.pallas_call(functools.partial(kernel, dims), out_shape=jax.ShapeDtypeS...  76.9 us
    unnamed x26, local copies, waits for them, and re-layouts  10.2 us

profile of v1, /device:TPU:1, one launch (start us, length us, event | category | flops | bytes accessed | tf_op | source)
XLA Modules:
  0.0 90.7 jit_solution(14766279740869549318)
XLA Ops:
  1.9 0.0 copy-start.11
  1.9 0.0 copy-start.12
  1.9 0.7 copy-done.11
  2.6 0.0 copy-done.12
  2.6 0.0 copy-start
  2.6 1.1 %copy-done = bf16[1,2,2,32,3072]{4,3,2,1,0:T(8,128)(2,1)S(1)} copy-done((bf16[1,2,2,32,3072]{4,3,2,1,0:T(8,128)(2,1)S(1)}, bf16[1,2,2,32,3072]{4,3,2,1,0:T(8,128)(2,1)}, u32[]{:S(2)}) %copy-start) | copy-done | bytes 786456
  3.7 0.0 copy-start.1
  3.7 1.0 %copy-done.1 = bf16[1,2,2,32,1536]{4,3,2,1,0:T(8,128)(2,1)S(1)} copy-done((bf16[1,2,2,32,1536]{4,3,2,1,0:T(8,128)(2,1)S(1)}, bf16[1,2,2,32,1536]{4,3,2,1,0:T(8,128)(2,1)}, u32[]{:S(2)}) %copy-start.1) | copy-done | bytes 393240
  4.7 0.0 copy-start.2
  4.7 1.0 %copy-done.2 = bf16[1,2,2,32,1536]{4,3,2,1,0:T(8,128)(2,1)S(1)} copy-done((bf16[1,2,2,32,1536]{4,3,2,1,0:T(8,128)(2,1)S(1)}, bf16[1,2,2,32,1536]{4,3,2,1,0:T(8,128)(2,1)}, u32[]{:S(2)}) %copy-start.2) | copy-done | bytes 393240
  5.7 0.0 copy-start.3
  5.7 1.0 %copy-done.3 = bf16[1,2,2,32,1536]{4,3,2,1,0:T(8,128)(2,1)S(1)} copy-done((bf16[1,2,2,32,1536]{4,3,2,1,0:T(8,128)(2,1)S(1)}, bf16[1,2,2,32,1536]{4,3,2,1,0:T(8,128)(2,1)}, u32[]{:S(2)}) %copy-start.3) | copy-done | bytes 393240
  6.7 0.0 copy-start.4
  6.7 1.0 %copy-done.4 = bf16[3072,64]{0,1:T(8,128)(2,1)S(1)} copy-done((bf16[3072,64]{0,1:T(8,128)(2,1)S(1)}, bf16[3072,64]{0,1:T(8,128)(2,1)}, u32[]{:S(2)}) %copy-start.4) | copy-done | bytes 393240
  7.7 0.0 copy-start.6
  7.7 0.8 copy-done.6
  8.5 0.0 copy-start.7
  8.5 0.8 copy-done.7
  9.3 0.0 copy-start.8
  9.3 0.8 copy-done.8
  10.0 0.0 copy-start.9
  10.0 0.8 copy-done.9
  10.8 0.0 copy-start.10
  10.8 0.7 copy-done.10
  11.5 76.9 %step.1.packed = f32[144,128]{1,0:T(8,128)S(1)} custom-call(bf16[1,2,2,32,1536]{4,3,2,1,0:T(8,128)(2,1)S(1)} %copy-done.1, bf16[1,2,2,32,1536]{4,3,2,1,0:T(8,128)(2,1)S(1)} %copy-done.2, bf16[1,2,2,32,1536]{4,3,2,1,0:T(8,128)(2,1)S(1)} %copy-done.3, s32[3,12]{1,0:T(4,128)S(1)} %bitcast.9, bf16[64,96]{1,0:T(8,128)(2,1)S(1)} %bitcast.8, ...), custom_call_target="tpu_custom_call" | custom-call | tf_op jit(solution)/shard_map/step/pallas_call | solution.py:544
  88.4 0.0 copy-start.5
  88.4 0.6 copy-done.5
  89.0 1.7 %unpack.1 = (f32[64,96]{1,0:T(8,128)}, f32[64,192]{1,0:T(8,128)}) custom-call(f32[144,128]{1,0:T(8,128)} %copy-done.5), custom_call_target="tpu_custom_call" | custom-call | tf_op jit(solution)/shard_map/unpack/pallas_call | solution.py:589
Async XLA Ops:
  1.9 0.7 copy-start.11
  1.9 0.7 copy-start.12
  2.6 1.1 %copy-start = (bf16[1,2,2,32,3072]{4,3,2,1,0:T(8,128)(2,1)S(1)}, bf16[1,2,2,32,3072]{4,3,2,1,0:T(8,128)(2,1)}, u32[]{:S(2)}) copy-start(bf16[1,2,2,32,3072]{4,3,2,1,0:T(8,128)(2,1)} %st_hbm.1) | copy-start | bytes 2359300
  3.7 1.0 %copy-start.1 = (bf16[1,2,2,32,1536]{4,3,2,1,0:T(8,128)(2,1)S(1)}, bf16[1,2,2,32,1536]{4,3,2,1,0:T(8,128)(2,1)}, u32[]{:S(2)}) copy-start(bf16[1,2,2,32,1536]{4,3,2,1,0:T(8,128)(2,1)} %q_hbm.1) | copy-start | bytes 1179652
  4.7 1.0 %copy-start.2 = (bf16[1,2,2,32,1536]{4,3,2,1,0:T(8,128)(2,1)S(1)}, bf16[1,2,2,32,1536]{4,3,2,1,0:T(8,128)(2,1)}, u32[]{:S(2)}) copy-start(bf16[1,2,2,32,1536]{4,3,2,1,0:T(8,128)(2,1)} %k_hbm.1) | copy-start | bytes 1179652
  5.7 1.0 %copy-start.3 = (bf16[1,2,2,32,1536]{4,3,2,1,0:T(8,128)(2,1)S(1)}, bf16[1,2,2,32,1536]{4,3,2,1,0:T(8,128)(2,1)}, u32[]{:S(2)}) copy-start(bf16[1,2,2,32,1536]{4,3,2,1,0:T(8,128)(2,1)} %v_hbm.1) | copy-start | bytes 1179652
  6.7 1.0 %copy-start.4 = (bf16[3072,64]{0,1:T(8,128)(2,1)S(1)}, bf16[3072,64]{0,1:T(8,128)(2,1)}, u32[]{:S(2)}) copy-start(bf16[3072,64]{0,1:T(8,128)(2,1)} %param.22) | copy-start | bytes 1179652
  7.7 0.8 copy-start.6
  8.5 0.8 copy-start.7
  9.3 0.8 copy-start.8
  10.0 0.8 copy-start.9
  10.8 0.7 copy-start.10
  88.4 0.6 copy-start.5

commit v2 on v1

v2 whole, which is shorter than its diff:
```python
import functools
import math

import jax
import jax.numpy as jnp
from jax import lax
from jax.experimental import pallas as pl
from jax.experimental.pallas import tpu as pltpu
from jax.sharding import PartitionSpec as P

TILE_W = 8
COLS = 32
HEAD = 128
RANK = 64
LAT = 64
SAMPLER_STEP = -0.5
CLIP_RANGE = 0.2
NORM_EPS = 1e-06
HALF_LOG_TAU = 0.5 * math.log(2.0 * math.pi)
DOWN_SHARD = 96
UP_SHARD = 192
PIECE = 144
HALF = 80
FAR = 32768.0
F32 = jnp.float32
BF16 = jnp.bfloat16
MESH = pl.DeviceIdType.MESH


def dot(a, b, ca, cb):
    return lax.dot_general(a, b, (((ca,), (cb,)), ((), ())), preferred_element_type=F32)


def kernel(
    dims,
    q_hbm, k_hbm, v_hbm, win_hbm, a_hbm, b_hbm, st_hbm, mod_hbm, w_hbm, bias_hbm, lat_hbm, nxt_hbm,
    slp_hbm, adv_hbm,
    out,
    win, slp, adv, a_t, b_own, mod, bias, lat, nxt,
    q, kv, st, w_t, gath, a_full, b_full, att, even, rhs, pack, mate, chip, got, ysum, final,
    d2, dn, cross, offset, part_core, part_plane, load_sem, halo_send, halo_recv, g_send, g_recv, s_send, s_recv,
    r_send, r_recv,
):
    n_tm, n_h, n_g, n_z, heads, parts = dims
    width = heads * HEAD
    model = st.shape[-1]
    n_x = n_h // n_z
    tm, me_h, me_g = lax.axis_index("tm"), lax.axis_index("height"), lax.axis_index("group")
    core, z_lo = lax.rem(tm, 2), tm // 2
    me_x, me_z = me_h // n_z, lax.rem(me_h, n_z)
    half_h = n_h // 2
    me_h_odd = lax.rem(me_h, 2) == 1

    loads = [
        pltpu.make_async_copy(k_hbm.at[0], kv.at[0, 1:3, 1:3], load_sem.at[0]),
        pltpu.make_async_copy(v_hbm.at[0], kv.at[1, 1:3, 1:3], load_sem.at[1]),
        pltpu.make_async_copy(q_hbm.at[0], q, load_sem.at[2]),
        pltpu.make_async_copy(st_hbm.at[0], st, load_sem.at[3]),
        pltpu.make_async_copy(w_hbm, w_t, load_sem.at[4]),
    ]
    small = ((a_hbm, a_t), (b_hbm, b_own), (win_hbm, win), (mod_hbm, mod), (bias_hbm, bias), (lat_hbm, lat),
             (nxt_hbm, nxt), (slp_hbm, slp), (adv_hbm, adv))
    loads += [pltpu.make_async_copy(*ends, load_sem.at[5 + i]) for i, ends in enumerate(small)]
    first_loads, later_loads = (0, 1, 5, 6), (2, 3, 4, 7, 8, 9, 10, 11, 12, 13)
    for i in first_loads:
        loads[i].start()

    barrier = pltpu.get_barrier_semaphore()
    plane = 2 * n_h

    def greet_plane(i, _):
        at = lax.rem(me_h * 2 + z_lo + i, plane)
        pl.semaphore_signal(
            barrier, inc=1, device_id=(2 * lax.rem(at, 2) + core, at // 2, me_g), device_id_type=MESH
        )
        return 0

    lax.fori_loop(1, plane, greet_plane, 0)

    def greet_group(i, _):
        pl.semaphore_signal(
            barrier, inc=1, device_id=(tm, me_h, lax.rem(me_g + i, n_g)), device_id_type=MESH
        )
        return 0

    lax.fori_loop(1, n_g, greet_group, 0)
    for zl in range(2):
        pl.semaphore_signal(
            barrier, inc=1, device_id=(2 * zl + 1 - core, me_h, me_g), device_id_type=MESH
        )
        for step_h in (1, n_h - 1):
            pl.semaphore_signal(
                barrier, inc=1, device_id=(2 * zl + 1 - core, lax.rem(me_h + step_h, n_h), me_g),
                device_id_type=MESH,
            )

    lane = lax.broadcasted_iota(jnp.int32, (1, 128), 1)
    left = lane < 64
    unit_row = lax.broadcasted_iota(jnp.int32, (64, 128), 0)
    unit_lane = lax.broadcasted_iota(jnp.int32, (64, 128), 1)
    loads[5].wait()
    loads[6].wait()
    twice = (lax.rem(unit_lane, 64) == unit_row).astype(F32).astype(BF16)
    a_rows = dot(a_t[...], twice, 0, 0)
    b_wide = b_own[...].astype(F32)
    b_even, b_odd = b_wide[:, 0:128], b_wide[:, 64:192]
    edge = jnp.where(me_h_odd, b_wide[:, 0:64], b_wide[:, 128:192])
    own_rows = jnp.concatenate(
        [
            jnp.where(me_h_odd, b_odd, b_even),
            jnp.concatenate([edge[0:32], edge[32:64]], axis=1),
            jnp.where(left, a_rows[0:48], a_rows[48:96]),
        ],
        axis=0,
    ).astype(BF16)

    @pl.when(core == 0)
    def _():
        gath[me_h, 0:HALF, :] = own_rows[0:HALF]

    @pl.when(core == 1)
    def _():
        gath[me_h, HALF:PIECE, :] = own_rows[HALF:PIECE]

    first_tm, last_tm = tm == 0, tm == n_tm - 1
    first_h, last_h = me_h == 0, me_h == n_h - 1

    @pl.when(first_tm)
    def _():
        kv[:, 0:1] = jnp.zeros((2, 1, 4, COLS, width), BF16)

    @pl.when(last_tm)
    def _():
        kv[:, 3:4] = jnp.zeros((2, 1, 4, COLS, width), BF16)

    @pl.when(first_h)
    def _():
        kv[:, :, 0:1] = jnp.zeros((2, 4, 1, COLS, width), BF16)

    @pl.when(last_h)
    def _():
        kv[:, :, 3:4] = jnp.zeros((2, 4, 1, COLS, width), BF16)

    loads[0].wait()
    loads[1].wait()
    pl.semaphore_wait(barrier, plane - 1 + n_g - 1 + 6)

    n_parts = len(parts)
    firsts = [sum(parts[:i]) for i in range(n_parts + 1)]
    ahead_h = (tm, jnp.minimum(me_h + 1, n_h - 1), me_g)
    back_h = (tm, jnp.maximum(me_h - 1, 0), me_g)
    ahead_tm = (jnp.minimum(tm + 1, n_tm - 1), me_h, me_g)
    back_tm = (jnp.maximum(tm - 1, 0), me_h, me_g)

    def lanes(i, size):
        return pl.ds(pl.multiple_of(i * size, 128), size)

    def halo(part, way):
        cols = pl.ds(firsts[part] * HEAD, parts[part] * HEAD)
        src, dst, to = {
            0: (kv.at[:, 1:3, 2, :, cols], kv.at[:, 1:3, 0, :, cols], ahead_h),
            1: (kv.at[:, 1:3, 1, :, cols], kv.at[:, 1:3, 3, :, cols], back_h),
            2: (kv.at[:, 2, 1:3, :, cols], kv.at[:, 0, 1:3, :, cols], ahead_tm),
            3: (kv.at[:, 1, 1:3, :, cols], kv.at[:, 3, 1:3, :, cols], back_tm),
            4: (kv.at[:, 2, 0, :, cols], kv.at[:, 0, 0, :, cols], ahead_tm),
            5: (kv.at[:, 1, 0, :, cols], kv.at[:, 3, 0, :, cols], back_tm),
            6: (kv.at[:, 2, 3, :, cols], kv.at[:, 0, 3, :, cols], ahead_tm),
            7: (kv.at[:, 1, 3, :, cols], kv.at[:, 3, 3, :, cols], back_tm),
            8: (kv.at[:, 2, 2, :, cols], kv.at[:, 0, 0, :, cols], (ahead_tm[0], ahead_h[1], me_g)),
            9: (kv.at[:, 1, 2, :, cols], kv.at[:, 3, 0, :, cols], (back_tm[0], ahead_h[1], me_g)),
            10: (kv.at[:, 2, 1, :, cols], kv.at[:, 0, 3, :, cols], (ahead_tm[0], back_h[1], me_g)),
            11: (kv.at[:, 1, 1, :, cols], kv.at[:, 3, 3, :, cols], (back_tm[0], back_h[1], me_g)),
        }[way]
        return pltpu.make_async_remote_copy(
            src_ref=src, dst_ref=dst, send_sem=halo_send.at[part, way], recv_sem=halo_recv.at[part, way],
            device_id=to, device_id_type=MESH,
        )

    not_first_tm, not_last_tm = tm > 0, tm < n_tm - 1
    not_first_h, not_last_h = me_h > 0, me_h < n_h - 1
    sends = {
        0: not_last_h, 1: not_first_h, 2: not_last_tm, 3: not_first_tm,
        4: not_first_h & not_last_tm, 5: not_first_h & not_first_tm,
        6: not_last_h & not_last_tm, 7: not_last_h & not_first_tm,
        8: not_last_h & not_last_tm, 9: not_last_h & not_first_tm,
        10: not_first_h & not_last_tm, 11: not_first_h & not_first_tm,
    }
    receives = {
        0: not_first_h, 1: not_last_h, 2: not_first_tm, 3: not_last_tm,
        4: not_first_h & not_first_tm, 5: not_first_h & not_last_tm,
        6: not_last_h & not_first_tm, 7: not_last_h & not_last_tm,
        8: not_first_h & not_first_tm, 9: not_first_h & not_last_tm,
        10: not_last_h & not_first_tm, 11: not_last_h & not_last_tm,
    }

    def when_each(table, ways, part, act):
        for way in ways:
            @pl.when(table[way])
            def _(way=way):
                act(halo(part, way))

    def first_ways(part):
        return (0, 1, 2, 3) + ((8, 9, 10, 11) if part == n_parts - 1 else ())

    def second_ways(part):
        return () if part == n_parts - 1 else (4, 5, 6, 7)

    def late_ways(part):
        return (2, 3) + (second_ways(part) or (8, 9, 10, 11))

    def leave():
        for part in range(n_parts):
            when_each(sends, first_ways(part) + second_ways(part), part, lambda copy: copy.wait_send())

    my_rows = pl.ds(pl.multiple_of(core * HALF, 16), HALF)

    def gather_z(i):
        src = gath.at[me_h, my_rows]
        to = (tm, me_x * n_z + lax.rem(me_z + i, n_z), me_g)
        return pltpu.make_async_remote_copy(
            src_ref=src, dst_ref=src, send_sem=g_send.at[i], recv_sem=g_recv.at[0],
            device_id=to, device_id_type=MESH,
        )

    def gather_x(i):
        src = gath.at[pl.ds(me_x * n_z, n_z), my_rows]
        to = (tm, lax.rem(me_x + i, n_x) * n_z + me_z, me_g)
        return pltpu.make_async_remote_copy(
            src_ref=src, dst_ref=src, send_sem=g_send.at[n_z + i], recv_sem=g_recv.at[1],
            device_id=to, device_id_type=MESH,
        )

    def gather_core():
        src = gath.at[:, my_rows]
        return pltpu.make_async_remote_copy(
            src_ref=src, dst_ref=src, send_sem=g_send.at[0], recv_sem=g_recv.at[2],
            device_id=(2 * z_lo + 1 - core, me_h, me_g), device_id_type=MESH,
        )

    for i in range(1, n_z):
        gather_z(i).start()

    for part in range(n_parts):
        when_each(sends, first_ways(part), part, lambda copy: copy.start())
    for i in later_loads:
        loads[i].start()

    tokens = 4 * COLS
    q_at = lax.broadcasted_iota(jnp.int32, (tokens, 128), 0)
    feature = lax.broadcasted_iota(jnp.int32, (tokens, 128), 1)
    q_frame, q_row, q_tile = q_at // 64, lax.rem(q_at // 32, 2), lax.rem(q_at, 32) // TILE_W
    frame_at = tm * 2 - 1 + feature
    row_at = me_h * 2 - 1 + (feature - 4)
    gap_frame = jnp.where(
        (frame_at >= 0) & (frame_at < 2 * n_tm), jnp.abs(q_frame + 1 - feature), 99
    )
    gap_row = jnp.where(
        (row_at >= 0) & (row_at < 2 * n_h), jnp.abs(q_row + 1 - (feature - 4)), 99
    )
    gap_tile = jnp.abs(q_tile - (feature - 8))
    gap = jnp.where(
        feature < 4, gap_frame,
        jnp.where(feature < 8, gap_row, jnp.where(feature < 12, gap_tile, -1)),
    )
    k_at = lax.broadcasted_iota(jnp.int32, (512, 128), 0)
    k_feature = lax.broadcasted_iota(jnp.int32, (512, 128), 1)
    k_one_hot = (
        (k_feature == k_at // 128)
        | (k_feature == 4 + lax.rem(k_at // 32, 4))
        | (k_feature == 8 + lax.rem(k_at, 32) // TILE_W)
    ).astype(F32).astype(BF16)
    ones = jnp.ones((512, 128), BF16)
    factor = HEAD**-0.5 * math.log2(math.e)

    def attend(part):
        for head in range(firsts[part], firsts[part + 1]):
            cols = pl.ds(head * HEAD, HEAD)
            reach = jnp.where(
                lane < 4, win[0, head], jnp.where(lane < 8, win[1, head], win[2, head])
            )
            penalty = jnp.where(gap > reach, -FAR, 0.0).astype(BF16)
            query = jnp.concatenate([q[:, :, :, cols].reshape(tokens, HEAD), penalty], axis=1)
            key = jnp.concatenate([kv[0, :, :, :, cols].reshape(512, HEAD), k_one_hot], axis=1)
            scores = dot(query, key, 1, 1)
            top = jnp.max(scores, axis=1, keepdims=True)
            terms = jnp.exp2((scores - top) * factor).astype(BF16)
            value = jnp.concatenate([kv[1, :, :, :, cols].reshape(512, HEAD), ones], axis=1)
            mixed = dot(terms, value, 1, 0)
            att[:, cols] = (mixed[:, :HEAD] / mixed[:, HEAD:]).astype(BF16)

    step = 2 * UP_SHARD
    n_pairs = model // step

    def unrolled(carry, act):
        for i in range(n_pairs):
            carry = act(i, pl.ds(i * step, step), carry)
        return carry

    def sweep(carry, act):
        return lax.fori_loop(0, n_pairs, lambda i, c: act(i, lanes(i, step), c), carry)

    def fold(x):
        total = x[:, 0:128]
        for i in range(1, x.shape[1] // 128):
            total = total + x[:, i * 128 : (i + 1) * 128]
        return total

    def mean(total):
        return jnp.sum(total, axis=1, keepdims=True) * (1.0 / model)

    def prepare():
        def sums(_, cols, carry):
            sum_s, sum_w, sum_b, sum_c = carry
            wide = w_t[:, cols].astype(F32)
            return (
                sum_s + fold(st[:, :, :, cols].reshape(tokens, step).astype(F32)),
                sum_w + fold(wide * (1.0 + mod[2, :, cols])),
                sum_b + fold(b_full[:, cols].astype(F32) * mod[0, :, cols]),
                sum_c + fold(wide * mod[1, :, cols]),
            )

        narrow = jnp.zeros((LAT, 128), F32)
        sum_s, sum_w, sum_b, sum_c = sweep((jnp.zeros((tokens, 128), F32), narrow, narrow, narrow), sums)
        mean_s, mean_w, mean_b = mean(sum_s), mean(sum_w), mean(sum_b)

        def centre(_, cols, product):
            even[:, cols] = st[:, :, :, cols].reshape(tokens, step).astype(F32) - mean_s
            scaled_w = (w_t[:, cols].astype(F32) * (1.0 + mod[2, :, cols]) - mean_w).astype(BF16)
            scaled_b = (b_full[:, cols].astype(F32) * mod[0, :, cols] - mean_b).astype(BF16)
            rhs[0:64, cols] = scaled_w
            rhs[64:128, cols] = scaled_b
            return product + dot(scaled_w, scaled_b, 1, 1)

        cross[:, 0:RANK] = sweep(jnp.zeros((LAT, RANK), F32), centre).astype(BF16)
        constant = jnp.sum(sum_c, axis=1, keepdims=True)
        shift = jnp.sum(jnp.where(unit_row == unit_lane, constant, 0.0), axis=0, keepdims=True)
        offset[...] = shift + jnp.concatenate([bias[...], jnp.zeros((1, 64), F32)], axis=1)

    last_cols = firsts[-2] * HEAD

    def spread_x():
        for i in range(1, n_z):
            gather_z(i).wait_send()
        taken = gath.at[pl.ds(0, n_z - 1), my_rows]
        pltpu.make_async_copy(taken, taken, g_recv.at[0]).wait()
        for i in range(1, n_x):
            gather_x(i).start()

    def spread_core():
        for i in range(1, n_x):
            gather_x(i).wait_send()
        taken = gath.at[pl.ds(0, (n_x - 1) * n_z), my_rows]
        pltpu.make_async_copy(taken, taken, g_recv.at[1]).wait()
        gather_core().start()

    def lay_out():
        gather_core().wait()
        for i in later_loads:
            if i not in (2, 7):
                loads[i].wait()

        def adapter(pair, _):
            for i in range(2):
                both = gath[2 * pair + i, 96:144, :]
                at = pl.multiple_of((2 * pair + i) * 96, 16)
                a_full[pl.ds(at, 48), :] = both
                a_full[pl.ds(at + 48, 48), 0:64] = both[:, 64:128]
            at = pl.multiple_of(pair * step, 128)
            b_full[:, pl.ds(at, 128)] = gath[2 * pair, 0:64, :]
            b_full[:, pl.ds(at + 256, 128)] = gath[2 * pair + 1, 0:64, :]
            first = gath[2 * pair, 64:96, :].astype(F32)
            second = gath[2 * pair + 1, 64:96, :].astype(F32)
            b_full[0:32, pl.ds(at + 128, 128)] = jnp.where(
                left, first, pltpu.roll(second, 64, 1)
            ).astype(BF16)
            b_full[32:64, pl.ds(at + 128, 128)] = jnp.where(
                left, pltpu.roll(first, 64, 1), second
            ).astype(BF16)
            return 0

        lax.fori_loop(0, half_h, adapter, 0)
        for f in range(2):
            for j in range(16):
                cols = pl.ds(j * 128, 128)
                d2[pl.ds(f * 32 + 2 * j, 2), :] = nxt[0, f, :, cols] - lat[0, f, :, cols]
        for f in range(2):
            for r in range(2):
                pair = d2[pl.ds(f * 32 + r, 16, stride=2), :]
                dn[pl.ds(f * 64 + r * 32, 16, stride=2), :] = pair
                dn[pl.ds(f * 64 + r * 32 + 1, 16, stride=2), :] = pltpu.roll(pair, 64, 1)
        prepare()

    def arrive(part):
        when_each(receives, (0, 1), part, lambda copy: copy.wait_recv())
        when_each(sends, second_ways(part), part, lambda copy: copy.start())

    def finish_part(part):
        when_each(receives, late_ways(part), part, lambda copy: copy.wait_recv())
        attend(part)

    for i in (2, 7):
        loads[i].wait()
    arrive(0)
    spread_x()
    arrive(1)
    spread_core()
    for part in range(2, n_parts - 1):
        arrive(part)
    lay_out()
    for part in range(n_parts - 1):
        finish_part(part)
    low_sum = dot(att[:, 0:last_cols], a_full[0:last_cols, 0:64], 1, 0)
    arrive(n_parts - 1)
    finish_part(n_parts - 1)
    low = (low_sum + dot(att[:, last_cols:width], a_full[last_cols:width, 0:64], 1, 0)).astype(BF16)

    def forward(_, cols, carry):
        total, seen = carry
        apart = even[:, cols] + dot(low, rhs[64:128, cols], 1, 0)
        narrow = apart.astype(BF16)
        rhs[128:256, cols] = narrow
        return total + fold(apart * apart), seen + dot(narrow, rhs[0:128, cols], 1, 1)

    blank = jnp.zeros((tokens, 128), F32)
    total, seen = unrolled((blank, blank), forward)
    inverse = lax.rsqrt(mean(total) + NORM_EPS)
    by_weight = jnp.where(left, inverse * seen, 0.0)
    by_up = pltpu.roll(seen, 64, 1)[:, 0:64]
    residue = jnp.where(left, dn[...] - SAMPLER_STEP * (by_weight + offset[...]), 0.0)

    square = jnp.sum(jnp.sum(residue * residue, axis=0, keepdims=True), axis=1, keepdims=True)
    part_core[core] = jnp.broadcast_to(square, (8, 128))
    partner = (2 * z_lo + 1 - core, me_h, me_g)

    def sum_core():
        return pltpu.make_async_remote_copy(
            src_ref=part_core.at[core], dst_ref=part_core.at[core], send_sem=s_send.at[0], recv_sem=s_recv.at[0],
            device_id=partner, device_id_type=MESH,
        )

    sum_core().start()

    g_velocity = SAMPLER_STEP * residue
    along = inverse * (jnp.sum(g_velocity * by_weight, axis=1, keepdims=True) * (1.0 / model))
    by_token = (-(inverse * along) * low.astype(F32)).T.astype(BF16)
    by_lat = dot(low, (inverse * g_velocity).astype(BF16), 0, 0).astype(BF16)
    lhs = jnp.concatenate([by_lat, by_token], axis=1)

    def share_up(pair, cols, carry):
        up = mod[0, :, cols] * dot(lhs, rhs[:, cols], 1, 0)
        pack[pair, 0, 0:64, :] = up[:, 0:128].astype(BF16)
        pack[pair, 1, 0:64, :] = up[:, 256:384].astype(BF16)
        shared = up[:, 128:256]
        turned = pltpu.roll(shared, 64, 1)
        pack[pair, 0, 64:96, :] = jnp.where(left, shared[0:32], turned[32:64]).astype(BF16)
        pack[pair, 1, 64:96, :] = jnp.where(left, turned[0:32], shared[32:64]).astype(BF16)
        return carry

    unrolled(0, share_up)

    def to_mate(i):
        rows = (pl.ds(0, 96), pl.ds(96, 48))[i]
        return pltpu.make_async_remote_copy(
            src_ref=pack.at[:, 1 - core, rows], dst_ref=mate.at[:, rows],
            send_sem=r_send.at[i], recv_sem=r_recv.at[i], device_id=partner, device_id_type=MESH,
        )

    to_mate(0).start()
    g_low = inverse * (dot(g_velocity[:, 0:64].astype(BF16), cross[:, 0:RANK], 1, 0) - along * by_up)
    g_low_twice = jnp.concatenate([g_low, g_low], axis=1).astype(BF16)

    def share_down(pair, _):
        down = dot(att[:, pl.ds(pl.multiple_of(pair * 384, 128), 384)], g_low_twice, 0, 0)
        for i in range(4):
            top, low_end = down[i * 96 : i * 96 + 48], down[i * 96 + 48 : i * 96 + 96]
            pack[2 * pair + i // 2, i % 2, 96:144, :] = jnp.where(left, top, low_end).astype(BF16)
        return 0

    lax.fori_loop(0, half_h // 2, share_down, 0)
    to_mate(1).start()

    def add_mate(i):
        to_mate(i).wait()
        rows = (pl.ds(0, 96), pl.ds(96, 48))[i]

        def add(j, _):
            chip[j, rows, :] = (
                pack[j, core, rows, :].astype(F32) + mate[j, rows, :].astype(F32)
            ).astype(BF16)
            return 0

        lax.fori_loop(0, half_h, add, 0)

    takes = lax.rem(me_h, 2) == core
    slot = me_h * 2 + z_lo
    part_rows = (pl.ds(0, HALF), pl.ds(HALF, PIECE - HALF))

    def to_owner(i, zl):
        j = lax.rem(me_h // 2 + i, half_h)
        size = (HALF, PIECE - HALF)[zl]
        return pltpu.make_async_remote_copy(
            src_ref=chip.at[j, part_rows[zl]], dst_ref=got.at[slot, pl.ds(0, size)],
            send_sem=r_send.at[2 + 2 * i + zl], recv_sem=r_recv.at[2],
            device_id=(2 * zl + core, 2 * j + core, me_g), device_id_type=MESH,
        )

    def sum_owner(i, zl):
        j = lax.rem(me_h // 2 + i, half_h)
        return pltpu.make_async_remote_copy(
            src_ref=part_plane.at[slot], dst_ref=part_plane.at[slot], send_sem=s_send.at[1 + 2 * i + zl],
            recv_sem=s_recv.at[1], device_id=(2 * zl + core, 2 * j + core, me_g), device_id_type=MESH,
        )

    def for_owners(zl, act):
        @pl.when(jnp.logical_not(takes & (z_lo == zl)))
        def _():
            act(0, zl)

        for i in range(1, half_h):
            act(i, zl)

    sum_core().wait()
    part_plane[slot] = part_core[0] + part_core[1]
    for zl in range(2):
        for_owners(zl, lambda i, zl: sum_owner(i, zl).start())

    for zl in range(2):
        add_mate(zl)
        own = takes & (z_lo == zl)

        @pl.when(own)
        def _(zl=zl):
            size = (HALF, PIECE - HALF)[zl]
            got[slot, 0:size, :] = chip[me_h // 2, part_rows[zl], :]

        for_owners(zl, lambda i, zl: to_owner(i, zl).start())

    def to_group(i):
        return pltpu.make_async_remote_copy(
            src_ref=ysum.at[me_g], dst_ref=ysum.at[me_g], send_sem=r_send.at[2 + n_h + i], recv_sem=r_recv.at[3],
            device_id=(tm, me_h, lax.rem(me_g + i, n_g)), device_id_type=MESH,
        )

    def to_tm(i):
        there = lax.rem(tm + i, n_tm)
        return pltpu.make_async_remote_copy(
            src_ref=final.at[z_lo], dst_ref=final.at[z_lo], send_sem=r_send.at[2 + n_h + n_g + i],
            recv_sem=r_recv.at[4 + z_lo], device_id=(there, me_h, me_g), device_id_type=MESH,
        )

    @pl.when(takes)
    def _():
        arrived = part_plane.at[0 : plane - 1]
        pltpu.make_async_copy(arrived, arrived, s_recv.at[1]).wait()
        square = part_plane[0]
        for i in range(1, plane):
            square = square + part_plane[i]
        square = square[0:1, :]
        count = 4 * COLS * LAT * n_tm * n_h
        logp = -square / (2.0 * count) - HALF_LOG_TAU
        gain = adv[0]
        ratio = jnp.exp(logp - slp[0])
        low_end, high_end = 1.0 - CLIP_RANGE, 1.0 + CLIP_RANGE
        plain = -gain * ratio
        cut = -gain * jnp.clip(ratio, low_end, high_end)
        inside = jnp.where(
            (ratio > low_end) & (ratio < high_end), 1.0,
            jnp.where((ratio == low_end) | (ratio == high_end), 0.5, 0.0),
        )
        weight = jnp.where(plain > cut, 1.0, jnp.where(plain == cut, 0.5 + 0.5 * inside, inside))
        slope = weight * plain * (1.0 / n_g)

        for zl in range(2):
            @pl.when(z_lo == zl)
            def _(zl=zl):
                arrived = got.at[0 : plane - 1, pl.ds(0, (HALF, PIECE - HALF)[zl])]
                pltpu.make_async_copy(arrived, arrived, r_recv.at[2]).wait()
        share = lax.fori_loop(
            0, plane // 4,
            lambda i, sofar: sofar
            + ((got[4 * i].astype(F32) + got[4 * i + 1].astype(F32))
               + (got[4 * i + 2].astype(F32) + got[4 * i + 3].astype(F32))),
            jnp.zeros((HALF, 128), F32),
        )
        ysum[me_g] = (share * slope).astype(BF16)
        for i in range(1, n_g):
            to_group(i).start()
        pltpu.make_async_copy(ysum.at[0 : n_g - 1], ysum.at[0 : n_g - 1], r_recv.at[3]).wait()
        share = ysum[0].astype(F32)
        for i in range(1, n_g):
            share = share + ysum[i].astype(F32)
        final[z_lo] = share
        for i in range(1, n_tm):
            to_tm(i).start()
        other = 1 - z_lo
        pltpu.make_async_copy(final.at[other], final.at[other], r_recv.at[4 + other]).wait()
        for i in range(1, n_g):
            to_group(i).wait_send()
        for i in range(1, n_tm):
            to_tm(i).wait_send()

    @pl.when(jnp.logical_not(takes))
    def _():
        for zl in range(2):
            pltpu.make_async_copy(final.at[zl], final.at[zl], r_recv.at[4 + zl]).wait()

    out[0:HALF, :] = final[0]
    out[HALF:PIECE, :] = final[1, 0 : PIECE - HALF, :]

    leave()
    for zl in range(2):
        for_owners(zl, lambda i, zl: (to_owner(i, zl).wait_send(), sum_owner(i, zl).wait_send()))


def unpack_kernel(packed, down_t, up):
    odd = lax.rem(lax.axis_index("height"), 2) == 1
    full = packed[0:64, :]
    rest = packed[64:96, :]
    narrow = jnp.concatenate([rest[:, 0:64], rest[:, 64:128]], axis=0)

    @pl.when(odd)
    def _():
        up[...] = jnp.concatenate([narrow, full], axis=1)

    @pl.when(jnp.logical_not(odd))
    def _():
        up[...] = jnp.concatenate([full, narrow], axis=1)

    down = packed[96:144, :]
    down = jnp.concatenate([down[:, 0:64], down[:, 64:128]], axis=0)
    down_t[...] = down.T


def body(
    queries, keys, values, window, adapter_down_factor, adapter_up_factor, stream, modulation,
    closing_weight, closing_bias, latent, next_latent_sample, sampling_log_probability, advantage,
):
    heads = window.shape[0]
    width = heads * HEAD
    model = stream.shape[-1]
    n_tm, n_h, n_g = lax.axis_size("tm"), lax.axis_size("height"), lax.axis_size("group")
    n_z = 4 if n_h == 16 else 2
    parts = (4, 4, 3, 1) if heads == 12 else (1,) * heads
    dims = (n_tm, n_h, n_g, n_z, heads, parts)
    n_parts = len(parts)
    tokens = 4 * COLS
    vmem = pl.BlockSpec(memory_space=pltpu.VMEM)
    hbm = pl.BlockSpec(memory_space=pl.ANY)
    dma = pltpu.SemaphoreType.DMA
    packed = pl.pallas_call(
        functools.partial(kernel, dims),
        out_shape=jax.ShapeDtypeStruct((PIECE, 128), F32),
        in_specs=[hbm] * 14,
        out_specs=vmem,
        scratch_shapes=[
            pltpu.SMEM((3, heads), jnp.int32),
            pltpu.SMEM((1,), F32),
            pltpu.SMEM((1,), F32),
            pltpu.VMEM((RANK, DOWN_SHARD), BF16),
            pltpu.VMEM((RANK, UP_SHARD), BF16),
            pltpu.VMEM((3, 1, model), F32),
            pltpu.VMEM((1, LAT), F32),
            pltpu.VMEM((1, 2, 2, COLS * LAT), F32),
            pltpu.VMEM((1, 2, 2, COLS * LAT), F32),
            pltpu.VMEM((2, 2, COLS, width), BF16),
            pltpu.VMEM((2, 4, 4, COLS, width), BF16),
            pltpu.VMEM((2, 2, COLS, model), BF16),
            pltpu.VMEM((LAT, model), BF16),
            pltpu.VMEM((n_h, 2 * HALF, 128), BF16),
            pltpu.VMEM((width, 128), BF16),
            pltpu.VMEM((RANK, model), BF16),
            pltpu.VMEM((tokens, width), BF16),
            pltpu.VMEM((tokens, model), F32),
            pltpu.VMEM((256, model), BF16),
            pltpu.VMEM((n_h // 2, 2, PIECE, 128), BF16),
            pltpu.VMEM((n_h // 2, PIECE, 128), BF16),
            pltpu.VMEM((n_h // 2, PIECE, 128), BF16),
            pltpu.VMEM((2 * n_h, HALF, 128), BF16),
            pltpu.VMEM((n_g, HALF, 128), BF16),
            pltpu.VMEM((2, HALF, 128), F32),
            pltpu.VMEM((64, 128), F32),
            pltpu.VMEM((128, 128), F32),
            pltpu.VMEM((LAT, 128), BF16),
            pltpu.VMEM((1, 128), F32),
            pltpu.VMEM((2, 8, 128), F32),
            pltpu.VMEM((2 * n_h, 8, 128), F32),
            dma((14,)),
            dma((n_parts, 12)),
            dma((n_parts, 12)),
            dma((n_h,)),
            dma((3,)),
            dma((1 + n_h,)),
            dma((2,)),
            dma((2 + n_h + n_g + n_tm,)),
            dma((6,)),
        ],
        compiler_params=pltpu.CompilerParams(
            collective_id=0, has_side_effects=True, vmem_limit_bytes=63 * 1024 * 1024
        ),
        name="step",
    )(
        queries, keys, values, window.T, adapter_down_factor.T, adapter_up_factor, stream,
        modulation.transpose(1, 0, 2), closing_weight.T, closing_bias.reshape(1, LAT), latent,
        next_latent_sample, sampling_log_probability, advantage,
    )
    down_t, up = pl.pallas_call(
        unpack_kernel,
        out_shape=(
            jax.ShapeDtypeStruct((RANK, DOWN_SHARD), F32),
            jax.ShapeDtypeStruct((RANK, UP_SHARD), F32),
        ),
        in_specs=[vmem],
        out_specs=(vmem, vmem),
        name="unpack",
    )(packed)
    return (down_t.T, up)


def solution(mesh):
    return jax.shard_map(
        body,
        mesh=mesh,
        in_specs=(
            P("group", "tm", "height", None, None),
            P("group", "tm", "height", None, None),
            P("group", "tm", "height", None, None),
            P(),
            P("height", None),
            P(None, "height"),
            P("group", "tm", "height", None, None),
            P("group", None, None),
            P(),
            P(),
            P("group", "tm", "height", None),
            P("group", "tm", "height", None),
            P("group"),
            P("group"),
        ),
        out_specs=(P("height", None), P(None, "height")),
        check_vma=False,
    )
```

time: 91.4 us -> 77.6 us (0.85)
  local copies, waits for them, and re-layouts: 10.2 us -> 0 us
  Pallas kernels: 78.6 us -> 75.5 us
    unnamed x26 -> x0, local copies, waits for them, and re-layouts: 10.2 us -> none
    pallas_call x1, Pallas kernels: 76.9 us -> 73.7 us  [body(): pl.pallas_call(functools.partial(kernel, dims), out_shape=jax.ShapeDtypeS...]
where the time goes in v2:
time: 77.6 us; the launch traced here: 77.4 us
  Pallas kernels  75.5 us (97%)
  between operations  1.93 us (2%)
    pallas_call x1, Pallas kernels, body(): pl.pallas_call(functools.partial(kernel, dims), out_shape=jax.ShapeDtypeS...  73.7 us
    pallas_call x1, Pallas kernels, body(): pl.pallas_call(unpack_kernel, out_shape=(jax.ShapeDtypeStruct((RANK, DOWN...  1.72 us

profile of v2, /device:TPU:1, one launch (start us, length us, event | category | flops | bytes accessed | tf_op | source)
XLA Modules:
  0.0 77.4 jit_solution(7856643938529803121)
XLA Ops:
  1.9 73.7 %step.1.packed = f32[144,128]{1,0:T(8,128)} custom-call(bf16[1,2,2,32,1536]{4,3,2,1,0:T(8,128)(2,1)} %q_hbm.1, bf16[1,2,2,32,1536]{4,3,2,1,0:T(8,128)(2,1)} %k_hbm.1, bf16[1,2,2,32,1536]{4,3,2,1,0:T(8,128)(2,1)} %v_hbm.1, s32[3,12]{1,0:T(4,128)} %bitcast.9, bf16[64,96]{1,0:T(8,128)(2,1)} %bitcast.8, bf16[64,192]{1,0:T(8,128)(2,1)} %b_hbm.1, ...), custom_call_target="tpu_custom_call" | custom-call | tf_op jit(solution)/shard_map/step/pallas_call | solution.py:650
  75.7 1.7 %unpack.1 = (f32[64,96]{1,0:T(8,128)}, f32[64,192]{1,0:T(8,128)}) custom-call(f32[144,128]{1,0:T(8,128)} %step.1.packed), custom_call_target="tpu_custom_call" | custom-call | tf_op jit(solution)/shard_map/unpack/pallas_call | solution.py:706

commit v3 on v2

--- a/solution.py
+++ b/solution.py
@@ -39,7 +39,7 @@
     win, slp, adv, a_t, b_own, mod, bias, lat, nxt,
     q, kv, st, w_t, gath, a_full, b_full, att, even, rhs, pack, mate, chip, got, ysum, final,
     d2, dn, cross, offset, part_core, part_plane, load_sem, halo_send, halo_recv, g_send, g_recv, s_send, s_recv,
-    r_send, r_recv,
+    r_send, r_recv, across,
 ):
     n_tm, n_h, n_g, n_z, heads, parts = dims
     width = heads * HEAD
@@ -68,14 +68,24 @@
     barrier = pltpu.get_barrier_semaphore()
     plane = 2 * n_h
 
-    def greet_plane(i, _):
-        at = lax.rem(me_h * 2 + z_lo + i, plane)
-        pl.semaphore_signal(
-            barrier, inc=1, device_id=(2 * lax.rem(at, 2) + core, at // 2, me_g), device_id_type=MESH
-        )
-        return 0
-
-    lax.fori_loop(1, plane, greet_plane, 0)
+    def greet(height, at_tm):
+        pl.semaphore_signal(barrier, inc=1, device_id=(at_tm, height, me_g), device_id_type=MESH)
+
+    for i in range(1, n_z):
+        greet(me_x * n_z + lax.rem(me_z + i, n_z), tm)
+    for i in range(1, n_x):
+        greet(lax.rem(me_x + i, n_x) * n_z + me_z, tm)
+    greet(me_h, lax.rem(tm + 2, n_tm))
+    crosses = (me_z == n_z - 1, me_z == 0)
+
+    @pl.when(crosses[0])
+    def _():
+        greet(lax.rem(me_h + 1, n_h), tm)
+
+    @pl.when(crosses[1])
+    def _():
+        greet(lax.rem(me_h + n_h - 1, n_h), tm)
+
 
     def greet_group(i, _):
         pl.semaphore_signal(
@@ -143,7 +153,8 @@
 
     loads[0].wait()
     loads[1].wait()
-    pl.semaphore_wait(barrier, plane - 1 + n_g - 1 + 6)
+    crossing = crosses[0].astype(jnp.int32) + crosses[1].astype(jnp.int32)
+    pl.semaphore_wait(barrier, n_z - 1 + n_x - 1 + 1 + n_g - 1 + 6 + crossing)
 
     n_parts = len(parts)
     firsts = [sum(parts[:i]) for i in range(n_parts + 1)]
@@ -310,31 +321,42 @@
 
     def prepare():
         def sums(_, cols, carry):
-            sum_s, sum_w, sum_b, sum_c = carry
+            sum_s, sum_w, sum_c = carry
             wide = w_t[:, cols].astype(F32)
             return (
                 sum_s + fold(st[:, :, :, cols].reshape(tokens, step).astype(F32)),
                 sum_w + fold(wide * (1.0 + mod[2, :, cols])),
-                sum_b + fold(b_full[:, cols].astype(F32) * mod[0, :, cols]),
                 sum_c + fold(wide * mod[1, :, cols]),
             )
 
         narrow = jnp.zeros((LAT, 128), F32)
-        sum_s, sum_w, sum_b, sum_c = sweep((jnp.zeros((tokens, 128), F32), narrow, narrow, narrow), sums)
-        mean_s, mean_w, mean_b = mean(sum_s), mean(sum_w), mean(sum_b)
-
-        def centre(_, cols, product):
+        sum_s, sum_w, sum_c = sweep((jnp.zeros((tokens, 128), F32), narrow, narrow), sums)
+        mean_s, mean_w = mean(sum_s), mean(sum_w)
+
+        def centre(_, cols, carry):
             even[:, cols] = st[:, :, :, cols].reshape(tokens, step).astype(F32) - mean_s
-            scaled_w = (w_t[:, cols].astype(F32) * (1.0 + mod[2, :, cols]) - mean_w).astype(BF16)
-            scaled_b = (b_full[:, cols].astype(F32) * mod[0, :, cols] - mean_b).astype(BF16)
-            rhs[0:64, cols] = scaled_w
-            rhs[64:128, cols] = scaled_b
-            return product + dot(scaled_w, scaled_b, 1, 1)
-
-        cross[:, 0:RANK] = sweep(jnp.zeros((LAT, RANK), F32), centre).astype(BF16)
+            rhs[0:64, cols] = (w_t[:, cols].astype(F32) * (1.0 + mod[2, :, cols]) - mean_w).astype(BF16)
+            return carry
+
+        sweep(0, centre)
         constant = jnp.sum(sum_c, axis=1, keepdims=True)
         shift = jnp.sum(jnp.where(unit_row == unit_lane, constant, 0.0), axis=0, keepdims=True)
         offset[...] = shift + jnp.concatenate([bias[...], jnp.zeros((1, 64), F32)], axis=1)
+
+    def prepare_up():
+        sum_b = sweep(
+            jnp.zeros((RANK, 128), F32),
+            lambda _, cols, total: total + fold(b_full[:, cols].astype(F32) * mod[0, :, cols]),
+        )
+        mean_b = mean(sum_b)
+
+        def centre(_, cols, product):
+            scaled = (b_full[:, cols].astype(F32) * mod[0, :, cols] - mean_b).astype(BF16)
+            rhs[64:128, cols] = scaled
+            return product + dot(rhs[0:64, cols], scaled, 1, 1)
+
+        cross[:, 0:RANK] = sweep(jnp.zeros((LAT, RANK), F32), centre).astype(BF16)
+
 
     last_cols = firsts[-2] * HEAD
 
@@ -351,13 +373,11 @@
             gather_x(i).wait_send()
         taken = gath.at[pl.ds(0, (n_x - 1) * n_z), my_rows]
         pltpu.make_async_copy(taken, taken, g_recv.at[1]).wait()
+        pl.semaphore_signal(across, inc=1, device_id=(lax.rem(tm + 2, n_tm), me_h, me_g), device_id_type=MESH)
         gather_core().start()
 
     def lay_out():
         gather_core().wait()
-        for i in later_loads:
-            if i not in (2, 7):
-                loads[i].wait()
 
         def adapter(pair, _):
             for i in range(2):
@@ -379,6 +399,12 @@
             return 0
 
         lax.fori_loop(0, half_h, adapter, 0)
+        prepare_up()
+
+    def differ():
+        for i in later_loads:
+            if i not in (2, 7):
+                loads[i].wait()
         for f in range(2):
             for j in range(16):
                 cols = pl.ds(j * 128, 128)
@@ -388,7 +414,6 @@
                 pair = d2[pl.ds(f * 32 + r, 16, stride=2), :]
                 dn[pl.ds(f * 64 + r * 32, 16, stride=2), :] = pair
                 dn[pl.ds(f * 64 + r * 32 + 1, 16, stride=2), :] = pltpu.roll(pair, 64, 1)
-        prepare()
 
     def arrive(part):
         when_each(receives, (0, 1), part, lambda copy: copy.wait_recv())
@@ -400,12 +425,13 @@
 
     for i in (2, 7):
         loads[i].wait()
+    differ()
+    prepare()
     arrive(0)
     spread_x()
     arrive(1)
     spread_core()
-    for part in range(2, n_parts - 1):
-        arrive(part)
+    arrive(2)
     lay_out()
     for part in range(n_parts - 1):
         finish_part(part)
@@ -519,6 +545,7 @@
         for i in range(1, half_h):
             act(i, zl)
 
+    pl.semaphore_wait(across, 1)
     sum_core().wait()
     part_plane[slot] = part_core[0] + part_core[1]
     for zl in range(2):
@@ -693,6 +720,7 @@
             dma((2,)),
             dma((2 + n_h + n_g + n_tm,)),
             dma((6,)),
+            pltpu.SemaphoreType.REGULAR,
         ],
         compiler_params=pltpu.CompilerParams(
             collective_id=0, has_side_effects=True, vmem_limit_bytes=63 * 1024 * 1024

time: 77.6 us -> 76.3 us (0.983)
  Pallas kernels: 75.5 us -> 74.2 us
    pallas_call x1, Pallas kernels: 73.7 us -> 72.4 us  [body(): pl.pallas_call(functools.partial(kernel, dims), out_shape=jax.ShapeDtypeS...]
where the time goes in v3:
time: 76.3 us; the launch traced here: 76.1 us
  Pallas kernels  74.2 us (97%)
  between operations  1.93 us (3%)
    pallas_call x1, Pallas kernels, body(): pl.pallas_call(functools.partial(kernel, dims), out_shape=jax.ShapeDtypeS...  72.4 us
    pallas_call x1, Pallas kernels, body(): pl.pallas_call(unpack_kernel, out_shape=(jax.ShapeDtypeStruct((RANK, DOWN...  1.72 us

profile of v3, /device:TPU:1, one launch (start us, length us, event | category | flops | bytes accessed | tf_op | source)
XLA Modules:
  0.0 76.1 jit_solution(13096809272593119737)
XLA Ops:
  1.9 72.4 %step.1.packed = f32[144,128]{1,0:T(8,128)} custom-call(bf16[1,2,2,32,1536]{4,3,2,1,0:T(8,128)(2,1)} %q_hbm.1, bf16[1,2,2,32,1536]{4,3,2,1,0:T(8,128)(2,1)} %k_hbm.1, bf16[1,2,2,32,1536]{4,3,2,1,0:T(8,128)(2,1)} %v_hbm.1, s32[3,12]{1,0:T(4,128)} %bitcast.9, bf16[64,96]{1,0:T(8,128)(2,1)} %bitcast.8, bf16[64,192]{1,0:T(8,128)(2,1)} %b_hbm.1, ...), custom_call_target="tpu_custom_call" | custom-call | tf_op jit(solution)/shard_map/step/pallas_call | solution.py:677
  74.4 1.7 %unpack.1 = (f32[64,96]{1,0:T(8,128)}, f32[64,192]{1,0:T(8,128)}) custom-call(f32[144,128]{1,0:T(8,128)} %step.1.packed), custom_call_target="tpu_custom_call" | custom-call | tf_op jit(solution)/shard_map/unpack/pallas_call | solution.py:734

commit v4 on v3

--- a/solution.py
+++ b/solution.py
@@ -616,7 +616,7 @@
         share = ysum[0].astype(F32)
         for i in range(1, n_g):
             share = share + ysum[i].astype(F32)
-        final[z_lo] = share
+        final[z_lo] = share.astype(BF16)
         for i in range(1, n_tm):
             to_tm(i).start()
         other = 1 - z_lo
@@ -631,8 +631,8 @@
         for zl in range(2):
             pltpu.make_async_copy(final.at[zl], final.at[zl], r_recv.at[4 + zl]).wait()
 
-    out[0:HALF, :] = final[0]
-    out[HALF:PIECE, :] = final[1, 0 : PIECE - HALF, :]
+    out[0:HALF, :] = final[0].astype(F32)
+    out[HALF:PIECE, :] = final[1, 0 : PIECE - HALF, :].astype(F32)
 
     leave()
     for zl in range(2):
@@ -704,7 +704,7 @@
             pltpu.VMEM((n_h // 2, PIECE, 128), BF16),
             pltpu.VMEM((2 * n_h, HALF, 128), BF16),
             pltpu.VMEM((n_g, HALF, 128), BF16),
-            pltpu.VMEM((2, HALF, 128), F32),
+            pltpu.VMEM((2, HALF, 128), BF16),
             pltpu.VMEM((64, 128), F32),
             pltpu.VMEM((128, 128), F32),
             pltpu.VMEM((LAT, 128), BF16),

time: 76.3 us -> 76 us (level)
  no operation moved by 1% of the time
where the time goes in v4:
time: 76 us; the launch traced here: 75.7 us
  Pallas kernels  73.8 us (97%)
  between operations  1.93 us (3%)
    pallas_call x1, Pallas kernels, body(): pl.pallas_call(functools.partial(kernel, dims), out_shape=jax.ShapeDtypeS...  72.1 us
    pallas_call x1, Pallas kernels, body(): pl.pallas_call(unpack_kernel, out_shape=(jax.ShapeDtypeStruct((RANK, DOWN...  1.72 us

profile of v4, /device:TPU:1, one launch (start us, length us, event | category | flops | bytes accessed | tf_op | source)
XLA Modules:
  0.0 75.7 jit_solution(1927892591655195482)
XLA Ops:
  1.9 72.1 %step.1.packed = f32[144,128]{1,0:T(8,128)} custom-call(bf16[1,2,2,32,1536]{4,3,2,1,0:T(8,128)(2,1)} %q_hbm.1, bf16[1,2,2,32,1536]{4,3,2,1,0:T(8,128)(2,1)} %k_hbm.1, bf16[1,2,2,32,1536]{4,3,2,1,0:T(8,128)(2,1)} %v_hbm.1, s32[3,12]{1,0:T(4,128)} %bitcast.9, bf16[64,96]{1,0:T(8,128)(2,1)} %bitcast.8, bf16[64,192]{1,0:T(8,128)(2,1)} %b_hbm.1, ...), custom_call_target="tpu_custom_call" | custom-call | tf_op jit(solution)/shard_map/step/pallas_call | solution.py:677
  74.0 1.7 %unpack.1 = (f32[64,96]{1,0:T(8,128)}, f32[64,192]{1,0:T(8,128)}) custom-call(f32[144,128]{1,0:T(8,128)} %step.1.packed), custom_call_target="tpu_custom_call" | custom-call | tf_op jit(solution)/shard_map/unpack/pallas_call | solution.py:734
